TPU v7x, 32 devices: a whole 2x2x4 slice. The times are simulated.
32 devices in a mesh: seq: 8 (over z, y), head: 4 (over x, core).
Axes of the slice: x: 2, y: 2, z: 4, core: 2. Of those that a mesh axis runs over, the one named last changes fastest.
Arguments:
- queries: bfloat16 [1, 4096, 1024], P(None, 'seq', 'head'), may hold values from -40 to 40
- key_vectors: bfloat16 [1, 4096, 1024], P(None, 'seq', 'head'), may hold values from -40 to 40
- value_vectors: bfloat16 [1, 4096, 1024], P(None, 'seq', 'head'), may hold values from -6 to 6
- out_weight: bfloat16 [1024, 1024], replicated, may hold values from -0.1875 to 0.1875
Outputs:
- layer_output: bfloat16 [1, 4096, 1024], P(None, ('seq', 'head'))
All inputs are finite; a program needn't handle non-finite values.
Results may differ from a plain program's by a relative error of at most 0.038.
Values may be sent and summed in bfloat16 or wider, within the bound.
No kernel may reach another device: no remote copies, remote signals or barrier semaphores. Data moves between devices by JAX's collectives and lax.ppermute only.
A program may use at most 192 MiB of HBM per device.

v0:
```python
import jax
import jax.numpy as jnp
from jax import lax
from jax.experimental import pallas as pl
from jax.experimental.pallas import tpu as pltpu
from jax.sharding import PartitionSpec as P

HD = 64
BLOCK = 128
LEVELS = 4
SLAB = 8
PAIR = 2 * HD

neg_fill = -1e30
root_half = 0.7071067811865476
log2_scale = HD**-0.5 * 1.4426950408889634

FAN = 2**LEVELS


def slabs_of(scratch, block):
    return [scratch[pl.ds(BLOCK * block + j, SLAB, stride=FAN), :] for j in range(FAN)]


def pooled_slabs(slabs):
    return [
        ((low + high) * root_half).astype(jnp.bfloat16).astype(jnp.float32)
        for low, high in zip(slabs[0::2], slabs[1::2])
    ]


def joined(slabs):
    return jnp.concatenate(slabs, axis=0).astype(jnp.bfloat16)


def spill(source, scratch):
    for half in range(scratch.shape[0]):
        scratch[half] = source[:, half * PAIR : (half + 1) * PAIR].astype(jnp.float32)


def pool_kernel(
    k_hbm, v_hbm, q_hbm, k_ref, v_ref, q_ref, first_ref, one_ref, two_ref, scratch, sems, q_sem
):
    rows = k_ref.shape[0]
    blocks = rows // BLOCK
    arrivals = []
    for block in range(blocks):
        here = pl.ds(block * BLOCK, BLOCK)
        for which, (source, target) in enumerate(((k_hbm, k_ref), (v_hbm, v_ref))):
            copy = pltpu.make_async_copy(
                source.at[0, here, :], target.at[here, :], sems.at[which, block]
            )
            copy.start()
            arrivals.append((block, which, target, copy))
    q_copy = pltpu.make_async_copy(q_hbm.at[0], q_ref, q_sem.at[0])
    q_copy.start()
    even = lax.rem(lax.axis_index("seq"), 2) == 0
    for block, which, ref, copy in arrivals:
        copy.wait()
        here = pl.ds(block * BLOCK, BLOCK)
        spill(ref.at[here, :], scratch.at[which, block])
        for half in range(scratch.shape[2]):
            lanes = pl.ds(half * PAIR, PAIR)
            one = pooled_slabs(slabs_of(scratch.at[which, block, half], 0))
            one_ref[which, pl.ds(block * BLOCK // 2, BLOCK // 2), lanes] = joined(one)
            two_ref[which, pl.ds(block * BLOCK // 4, BLOCK // 4), lanes] = joined(pooled_slabs(one))
    inner = rows // 4 - BLOCK // 4
    for which, ref in enumerate((k_ref, v_ref)):
        first_ref[which, :BLOCK, :] = jnp.where(even, ref[rows - BLOCK :, :], ref[:BLOCK, :])
        first_ref[which, BLOCK:, :] = jnp.where(
            even, two_ref[which, :inner, :], two_ref[which, BLOCK // 4 :, :]
        )
    q_copy.wait()


def repooled(field):
    rows, lanes = field.shape
    slabs = field.astype(jnp.float32).reshape(rows // (2 * SLAB), 2, SLAB, lanes)
    return ((slabs[:, 0] + slabs[:, 1]) * root_half).reshape(rows // 2, lanes).astype(jnp.bfloat16)


def deeper_kernel(k_ref, v_ref, two_ref, second_ref, three_ref, four_ref):
    rows = k_ref.shape[0]
    even = lax.rem(lax.axis_index("seq"), 2) == 0
    for which, ref in enumerate((k_ref, v_ref)):
        second_ref[which] = jnp.where(even, ref[:BLOCK, :], ref[rows - BLOCK :, :])
        three = repooled(two_ref[which])
        three_ref[which] = three
        four_ref[which] = repooled(three)


def repooled(field):
    rows, lanes = field.shape
    slabs = field.astype(jnp.float32).reshape(rows // (2 * SLAB), 2, SLAB, lanes)
    return ((slabs[:, 0] + slabs[:, 1]) * root_half).reshape(rows // 2, lanes).astype(jnp.bfloat16)


def score(queries, keys, hold, is_open=None):
    rows = queries.shape[0]
    low = lax.broadcasted_iota(jnp.int32, (rows, PAIR), 1) < HD
    zero = jnp.zeros_like(queries)
    both = jnp.concatenate([jnp.where(low, queries, zero), jnp.where(low, zero, queries)], axis=0)
    raw = lax.dot_general(both, keys, (((1,), (1,)), ((), ())), preferred_element_type=jnp.float32)
    if is_open is not None:
        raw = jnp.where(is_open, raw, neg_fill)
    hold[...] = raw
    return jnp.max(raw, axis=1, keepdims=True)


def weigh(hold, top, values):
    rows = top.shape[0] // 2
    low = lax.broadcasted_iota(jnp.int32, (rows, PAIR), 1) < HD
    weights = jnp.exp2((hold[...] - top) * log2_scale).astype(jnp.bfloat16)
    result = jnp.dot(weights, values, preferred_element_type=jnp.float32)
    return (
        log2_scale * jnp.where(low, top[:rows], top[rows:]),
        jnp.where(low, result[:rows, :PAIR], result[rows:, :PAIR]),
        jnp.where(low, result[:rows, PAIR:], result[rows:, PAIR:]),
    )


def merged(fine, coarse):
    top = jnp.maximum(fine[0], coarse[0])
    keep = jnp.exp2(fine[0] - top)
    join = jnp.exp2(coarse[0] - top)
    return top, fine[1] * keep + coarse[1] * join, fine[2] * keep + coarse[2] * join


def doubled(field):
    rows, lanes = field.shape
    slabs = field.reshape(rows // SLAB, 1, SLAB, lanes)
    return jnp.broadcast_to(slabs, (rows // SLAB, 2, SLAB, lanes)).reshape(2 * rows, lanes)


def with_ones(values, weight=1.0):
    if weight != 1.0:
        values = values * jnp.bfloat16(weight)
    return jnp.concatenate([values, jnp.full(values.shape, weight, jnp.bfloat16)], axis=1)


def local_kernel(
    q_ref, k_ref, v_ref, one_ref, four_ref, edge_q, two_q, three_q, four_q, state,
    scratch, near_hold, coarse_hold,
):
    rows = q_ref.shape[0]
    blocks = rows // BLOCK
    pairs = scratch.shape[0]
    spill(q_ref, scratch)
    fine, one_q = [], []
    for pair in range(pairs):
        lanes = pl.ds(pair * PAIR, PAIR)
        ladder = [[], [], [], [], []]
        for block in range(blocks):
            slabs = slabs_of(scratch.at[pair], block)
            ladder[0].append(joined(slabs))
            for level in range(1, LEVELS + 1):
                slabs = pooled_slabs(slabs)
                ladder[level] += slabs
        edge_q[0, :, lanes] = ladder[0][0]
        edge_q[1, :, lanes] = ladder[0][-1]
        two_q[:, lanes] = joined(ladder[2])
        three_q[:, lanes] = joined(ladder[3])
        four_q[:, lanes] = joined(ladder[4])
        fine.append(ladder[0])
        one_q.append([joined(ladder[1][n : n + FAN]) for n in range(0, len(ladder[1]), FAN)])
    windows = [(max(n - 1, 0) * BLOCK, min(n + 2, blocks) * BLOCK) for n in range(blocks)]
    tops = {}
    for pair in range(pairs):
        lanes = pl.ds(pair * PAIR, PAIR)
        for half in range(blocks // 2):
            there = pl.ds((half ^ 1) * BLOCK, BLOCK)
            tops[pair, half] = score(
                one_q[pair][half], one_ref[0, there, lanes], coarse_hold.at[pair, half]
            )
            for block in (2 * half, 2 * half + 1):
                low, high = windows[block]
                hold = near_hold.at[pair, block, :, : high - low]
                tops[pair, half, block] = score(fine[pair][block], k_ref[low:high, lanes], hold)
    for pair in range(pairs):
        lanes = pl.ds(pair * PAIR, PAIR)
        for half in range(blocks // 2):
            there = pl.ds((half ^ 1) * BLOCK, BLOCK)
            coarse = weigh(
                coarse_hold.at[pair, half], tops[pair, half], with_ones(one_ref[1, there, lanes])
            )
            for block in (2 * half, 2 * half + 1):
                low, high = windows[block]
                hold = near_hold.at[pair, block, :, : high - low]
                near = weigh(hold, tops[pair, half, block], with_ones(v_ref[low:high, lanes]))
                part = slice((block - 2 * half) * BLOCK // 2, (block - 2 * half + 1) * BLOCK // 2)
                done = merged(near, [doubled(x[part]) for x in coarse])
                for index, field in enumerate(done):
                    state[index, block * BLOCK : (block + 1) * BLOCK, lanes] = field


def join_kernel(four_ref, six_ref, query_ref, out):
    sixteenth = four_ref.shape[1]
    out[:, :sixteenth, :] = four_ref[...]
    out[:, sixteenth:, :] = six_ref[...]


def coarse_kernel(
    two_q, three_q, first_ref, three_a, three_b, coarse, near_ref, scratch, two_ref, two_hold, three_hold
):
    inner = first_ref.shape[1] - BLOCK
    pairs = scratch.shape[1]
    two_ref[:, :inner, :] = first_ref[:, BLOCK:, :]
    for which in range(2):
        spill(first_ref.at[which, pl.ds(0, BLOCK), :], scratch.at[which])
        for half in range(pairs):
            lanes = pl.ds(half * PAIR, PAIR)
            slabs = slabs_of(scratch.at[which, half], 0)
            two_ref[which, inner:, lanes] = joined(pooled_slabs(pooled_slabs(slabs)))
        near_ref[which] = repooled(repooled(two_ref[which]))
    steps = {}
    for pair in range(pairs):
        lanes = pl.ds(pair * PAIR, PAIR)
        three = [
            jnp.concatenate([three_a[which, :, lanes], three_b[which, :, lanes]], axis=0)
            for which in range(2)
        ]
        steps[pair, 3] = (
            score(three_q[:, lanes], three[0], three_hold.at[pair]), with_ones(three[1])
        )
        steps[pair, 2] = (
            score(two_q[:, lanes], two_ref[0, :, lanes], two_hold.at[pair]),
            with_ones(two_ref[1, :, lanes]),
        )
    for pair in range(pairs):
        three = weigh(three_hold.at[pair], *steps[pair, 3])
        two = merged(weigh(two_hold.at[pair], *steps[pair, 2]), [doubled(x) for x in three])
        for index, field in enumerate(two):
            coarse[index, :, pl.ds(pair * PAIR, PAIR)] = field


def mid_kernel(edge_q, coarse, state, first_ref, second_ref, out, holds):
    rows = state.shape[1]
    blocks = rows // BLOCK
    position = lax.axis_index("seq")
    last = lax.axis_size("seq") - 1
    even = lax.rem(position, 2) == 0
    opens = (position > 0, position < last)
    pairs = holds.shape[0]
    steps = {}
    for pair in range(pairs):
        lanes = pl.ds(pair * PAIR, PAIR)
        inner = [first_ref[which, :BLOCK, lanes] for which in range(2)]
        outer = [second_ref[which, :, lanes] for which in range(2)]
        for side in range(2):
            halo = [
                jnp.where(even, *((outer[which], inner[which])[:: 1 - 2 * side]))
                for which in range(2)
            ]
            steps[pair, side] = (
                score(edge_q[side, :, lanes], halo[0], holds.at[pair, side], opens[side]),
                with_ones(halo[1]),
            )
    for pair in range(pairs):
        lanes = pl.ds(pair * PAIR, PAIR)
        for block in range(blocks):
            here = slice(block * BLOCK, (block + 1) * BLOCK)
            quarter = slice(block * BLOCK // 4, (block + 1) * BLOCK // 4)
            done = merged(
                [state[index, here, lanes] for index in range(3)],
                [doubled(doubled(coarse[index, quarter, lanes])) for index in range(3)],
            )
            for side, edge in enumerate((0, blocks - 1)):
                if block == edge:
                    done = merged(done, weigh(holds.at[pair, side], *steps[pair, side]))
            for index, field in enumerate(done):
                out[index, here, lanes] = field


def finish_kernel(
    four_q, state, four_ref, near_ref, three_a, three_b, fours_a, fours_b, *refs
):
    far, refs = refs[:-6], refs[-6:]
    outs, (attended, four_hold) = refs[:-2], refs[-2:]
    rows = state.shape[1]
    blocks = rows // BLOCK
    own = lax.axis_index("head")
    pairs = four_q.shape[1] // PAIR
    steps = {}
    for pair in range(pairs):
        lanes = pl.ds(pair * PAIR, PAIR)
        ours, theirs, beyond = [], [], []
        for which in range(2):
            ours.append(
                [four_ref[which, :, lanes], near_ref[which, :, lanes]]
                + [repooled(field[which, :, lanes]) for field in (three_a, three_b)]
            )
            theirs.append([field[which, :, lanes] for field in (fours_a, fours_b)])
            beyond.append([field[which, :, lanes] for field in far])
        steps[pair] = (
            score(
                four_q[:, lanes],
                jnp.concatenate(ours[0] + theirs[0] + beyond[0], axis=0),
                four_hold.at[pair],
            ),
            jnp.concatenate(
                [with_ones(field) for field in ours[1]]
                + [with_ones(field, 2.0) for field in theirs[1]]
                + [with_ones(field) for field in beyond[1]],
                axis=0,
            ),
        )
    for pair in range(pairs):
        lanes = pl.ds(pair * PAIR, PAIR)
        four = weigh(four_hold.at[pair], *steps[pair])
        for block in range(blocks):
            here = slice(block * BLOCK, (block + 1) * BLOCK)
            coarse = [x[block * SLAB : (block + 1) * SLAB] for x in four]
            for _ in range(LEVELS):
                coarse = [doubled(x) for x in coarse]
            _, numer, rowsum = merged([state[index, here, lanes] for index in range(3)], coarse)
            attended[block, :, lanes] = (numer / rowsum).astype(jnp.bfloat16)
    for step, out in enumerate(outs):
        out[...] = attended[own ^ step]


def partial_kernel(near_ref, next_ref, weight_ref, out_ref):
    own = lax.axis_index("head")
    features = near_ref.shape[1]
    total = None
    for step, part in enumerate((near_ref, next_ref)):
        start = pl.multiple_of((own ^ step) * features, features)
        product = jnp.dot(
            part[...], weight_ref[pl.ds(start, features), :], preferred_element_type=jnp.float32
        )
        total = product if total is None else total + product
    out_ref[...] = total


def project_kernel(partial_ref, *refs):
    parts, (weight_ref, out_hbm, scratch, staged, sems) = refs[:-5], refs[-5:]
    own = lax.axis_index("head")
    features = parts[0].shape[1]
    chunk = staged.shape[2]
    copies = []
    for index in range(staged.shape[0]):
        columns = pl.ds(index * chunk, chunk)
        total = partial_ref[:, columns]
        for step, part in enumerate(parts, 2):
            start = pl.multiple_of((own ^ step) * features, features)
            total += jnp.dot(
                part[...],
                weight_ref[pl.ds(start, features), columns],
                preferred_element_type=jnp.float32,
            )
        for half in range(chunk // PAIR):
            lanes = slice(half * PAIR, (half + 1) * PAIR)
            scratch[index, half] = total[:, lanes]
            for i in range(SLAB):
                staged[index, i * FAN : (i + 1) * FAN, lanes] = scratch[
                    index, half, pl.ds(i, FAN, stride=SLAB), :
                ].astype(jnp.bfloat16)
        copy = pltpu.make_async_copy(staged.at[index], out_hbm.at[:, columns], sems.at[index])
        copy.start()
        copies.append(copy)
    for copy in copies:
        copy.wait()


def repool_outside(field):
    which, rows, lanes = field.shape
    slabs = field.astype(jnp.float32).reshape(which, rows // (2 * SLAB), 2, SLAB, lanes)
    sums = (slabs[:, :, 0] + slabs[:, :, 1]) * root_half
    return sums.reshape(which, rows // 2, lanes).astype(jnp.bfloat16)


def swapped(block, axis, mask):
    return lax.ppermute(block, axis, [(i, i ^ mask) for i in range(lax.axis_size(axis))])


def across(block):
    count, heads = lax.axis_size("seq"), lax.axis_size("head")
    route = []
    for seq in range(count):
        end = seq in (0, count - 1)
        other = seq if end else seq + 1 if seq % 2 else seq - 1
        for head in range(heads):
            route.append((seq * heads + head, other * heads + (head ^ 1 if end else head)))
    return lax.ppermute(block, ("seq", "head"), route)


def per_device(queries, key_vectors, value_vectors, out_weight):
    rows, features = queries.shape[1:]
    queries, key_vectors, value_vectors = [
        pltpu.with_memory_space_constraint(x, pltpu.HBM)
        for x in (queries, key_vectors, value_vectors)
    ]
    pairs = features // PAIR
    seq_count, head_count = lax.axis_size("seq"), lax.axis_size("head")
    bf16 = lambda *shape: jax.ShapeDtypeStruct(shape, jnp.bfloat16)
    params = pltpu.CompilerParams(vmem_limit_bytes=32 * 1024 * 1024)

    hbm = pl.BlockSpec(memory_space=pltpu.HBM)
    vmem = pl.BlockSpec(memory_space=pltpu.VMEM)
    keys, values, ours, first, one, two = pl.pallas_call(
        pool_kernel,
        in_specs=[hbm] * 3,
        out_shape=[
            bf16(rows, features),
            bf16(rows, features),
            bf16(rows, features),
            bf16(2, BLOCK + rows // 4 - BLOCK // 4, features),
            bf16(2, rows // 2, features),
            bf16(2, rows // 4, features),
        ],
        scratch_shapes=[
            pltpu.VMEM((2, rows // BLOCK, pairs, BLOCK, PAIR), jnp.float32),
            pltpu.SemaphoreType.DMA((2, rows // BLOCK)),
            pltpu.SemaphoreType.DMA((1,)),
        ],
        compiler_params=params,
        name="pool",
    )(key_vectors, value_vectors, queries)
    second, three, four = pl.pallas_call(
        deeper_kernel,
        out_shape=[
            bf16(2, BLOCK, features),
            bf16(2, rows // 8, features),
            bf16(2, rows // 16, features),
        ],
        compiler_params=params,
        cost_estimate=pl.CostEstimate(flops=2**31, bytes_accessed=2**23, transcendentals=0),
        name="deeper",
    )(keys, values, two)

    first_in = swapped(first, "seq", 1)
    second_in = across(second)
    four_in = swapped(four, "seq", 4)
    six_in = swapped(four, "seq", 6)
    threes_in = [swapped(three, "seq", mask) for mask in (3, 2)]
    edge_q, two_q, three_q, four_q, state = pl.pallas_call(
        local_kernel,
        out_shape=[
            bf16(2, BLOCK, features),
            bf16(rows // 4, features),
            bf16(rows // 8, features),
            bf16(rows // 16, features),
            jax.ShapeDtypeStruct((3, rows, features), jnp.float32),
        ],
        scratch_shapes=[
            pltpu.VMEM((pairs, rows, PAIR), jnp.float32),
            pltpu.VMEM((pairs, rows // BLOCK, 2 * BLOCK, 3 * BLOCK), jnp.float32),
            pltpu.VMEM((pairs, rows // BLOCK // 2, 2 * BLOCK, BLOCK), jnp.float32),
        ],
        compiler_params=params,
        name="local",
    )(ours, keys, values, one, four_in)

    fours = pl.pallas_call(
        join_kernel,
        out_shape=bf16(2, rows // 8, features),
        compiler_params=params,
        cost_estimate=pl.CostEstimate(flops=2**29, bytes_accessed=2**20, transcendentals=0),
        name="join",
    )(four_in, six_in, four_q)
    fours_in = swapped(fours, "seq", 1)
    coarse, near = pl.pallas_call(
        coarse_kernel,
        out_shape=[
            jax.ShapeDtypeStruct((3, rows // 4, features), jnp.float32),
            bf16(2, rows // 16, features),
        ],
        scratch_shapes=[
            pltpu.VMEM((2, pairs, BLOCK, PAIR), jnp.float32),
            pltpu.VMEM((2, rows // 4, features), jnp.bfloat16),
            pltpu.VMEM((pairs, rows // 2, BLOCK), jnp.float32),
            pltpu.VMEM((pairs, rows // 4, BLOCK), jnp.float32),
        ],
        compiler_params=params,
        cost_estimate=pl.CostEstimate(flops=2**31, bytes_accessed=2**21, transcendentals=0),
        name="coarse",
    )(two_q, three_q, first_in, *threes_in)
    state = pl.pallas_call(
        mid_kernel,
        out_shape=jax.ShapeDtypeStruct((3, rows, features), jnp.float32),
        input_output_aliases={2: 0},
        scratch_shapes=[pltpu.VMEM((pairs, 2, 2 * BLOCK, BLOCK), jnp.float32)],
        compiler_params=params,
        name="mid",
    )(edge_q, coarse, state, first_in, second_in)

    far = []
    known = 8
    if known < seq_count:
        group = [four, near] + [repool_outside(field) for field in threes_in]
        group = jnp.concatenate(group + [fours, fours_in], axis=1)
        while known < seq_count:
            fresh = swapped(group, "seq", known)
            far.append(fresh)
            group = jnp.concatenate([group, fresh], axis=1)
            known *= 2

    outs = pl.pallas_call(
        finish_kernel,
        out_shape=[bf16(BLOCK, features) for _ in range(head_count)],
        scratch_shapes=[
            pltpu.VMEM((rows // BLOCK, BLOCK, features), jnp.bfloat16),
            pltpu.VMEM((pairs, rows // 8, rows // 16 * seq_count), jnp.float32),
        ],
        compiler_params=params,
        name="finish",
    )(four_q, state, four, near, *threes_in, fours, fours_in, *far)

    parts = [part if step == 0 else swapped(part, "head", step) for step, part in enumerate(outs)]
    width = out_weight.shape[1]
    partial = pl.pallas_call(
        partial_kernel,
        out_shape=jax.ShapeDtypeStruct((BLOCK, width), jnp.float32),
        compiler_params=params,
        name="partial",
    )(*parts[:2], out_weight)
    chunk = 2 * PAIR
    result = pl.pallas_call(
        project_kernel,
        in_specs=[vmem] * len(parts),
        out_specs=hbm,
        out_shape=bf16(BLOCK, width),
        scratch_shapes=[
            pltpu.VMEM((width // chunk, 2, BLOCK, PAIR), jnp.float32),
            pltpu.VMEM((width // chunk, BLOCK, chunk), jnp.bfloat16),
            pltpu.SemaphoreType.DMA((width // chunk,)),
        ],
        compiler_params=params,
        name="project",
    )(partial, *parts[2:], out_weight)
    return result[None]


def solution(mesh):
    return jax.shard_map(
        per_device,
        mesh=mesh,
        in_specs=(P(None, "seq", "head"), P(None, "seq", "head"), P(None, "seq", "head"), P()),
        out_specs=P(None, ("seq", "head"), None),
        check_vma=False,
    )
```

profile of v0, /device:TPU:0, one launch (start us, length us, event | category | flops | bytes accessed | tf_op | source)
XLA Modules:
  0.0 24.8 jit_solution(15305998685672380875)
XLA Ops:
  0.0 1.4 %pool.1 = (bf16[512,256]{1,0:T(8,128)(2,1)S(1)}, bf16[512,256]{1,0:T(8,128)(2,1)S(1)}, bf16[512,256]{1,0:T(8,128)(2,1)S(1)}, bf16[2,224,256]{2,1,0:T(8,128)(2,1)...) custom-call(bf16[1,512,256]{2,1,0:T(8,128)(2,1)} %k_hbm.1, bf16[1,512,256]{2,1,0:T(8,128)(2,1)} %v_hbm.1, ...), custom_call_target="tpu_custom_call" | custom-call | tf_op jit(solution)/shard_map/pool/pallas_call | solution.py:399
  1.4 3.0 %collective-permute-start.1 = (bf16[2,224,256]{2,1,0:T(8,128)(2,1)S(1)}, bf16[2,224,256]{2,1,0:T(8,128)(2,1)S(1)}, u32[]{:S(2)}, u32[]{:S(2)}) collective-permute-start(bf16[2,224,256]{2,1,0:T(8,128)(2,1)S(1)} %get-tuple-element.35), channel_id=1, source_target_pairs={{0,4},{4,0},{8,12},{12,8},{16,20},{20,16},{24,28},{28,24},{1,5},{5... | collective-permute-start | bytes 688136 | tf_op jit(solution)/shard_map/ppermute | solution.py:372
  4.5 2.7 %collective-permute-start = (bf16[2,32,256]{2,1,0:T(8,128)(2,1)S(1)}, bf16[2,32,256]{2,1,0:T(8,128)(2,1)S(1)}, u32[]{:S(2)}, u32[]{:S(2)}) collective-permute-start(bf16[2,32,256]{2,1,0:T(8,128)(2,1)S(1)} %get-tuple-element.30.four_ref), channel_id=1, source_target_pairs={{0,16},{4,20},{8,24},{12,28},{16,0},{20,4},{24,8},{28,12},{1,17},{... | collective-permute-start | bytes 98312 | tf_op jit(solution)/shard_map/ppermute | solution.py:372
  7.2 1.3 %collective-permute-start.5 = (bf16[2,32,256]{2,1,0:T(8,128)(2,1)S(1)}, bf16[2,32,256]{2,1,0:T(8,128)(2,1)S(1)}, u32[]{:S(2)}, u32[]{:S(2)}) collective-permute-start(bf16[2,32,256]{2,1,0:T(8,128)(2,1)S(1)} %get-tuple-element.30.four_ref), channel_id=1, source_target_pairs={{0,24},{4,28},{8,16},{12,20},{16,8},{20,12},{24,0},{28,4},{1,25},{... | collective-permute-start | bytes 98312 | tf_op jit(solution)/shard_map/ppermute | solution.py:372
  8.5 0.2 collective-permute-start.2
  8.7 1.8 %collective-permute-start.3 = (bf16[2,64,256]{2,1,0:T(8,128)(2,1)S(1)}, bf16[2,64,256]{2,1,0:T(8,128)(2,1)S(1)}, u32[]{:S(2)}, u32[]{:S(2)}) collective-permute-start(bf16[2,64,256]{2,1,0:T(8,128)(2,1)S(1)} %get-tuple-element.36), channel_id=1, source_target_pairs={{0,8},{4,12},{8,0},{12,4},{16,24},{20,28},{24,16},{28,20},{1,9},{5... | collective-permute-start | bytes 196616 | tf_op jit(solution)/shard_map/ppermute | solution.py:372
  10.5 0.0 collective-permute-done.four_ref
  10.5 0.0 collective-permute-start.4
  10.5 1.5 %local.1 = (bf16[2,128,256]{2,1,0:T(8,128)(2,1)S(1)}, bf16[128,256]{1,0:T(8,128)(2,1)S(1)}, bf16[64,256]{1,0:T(8,128)(2,1)S(1)}, bf16[32,256]{1,0:T(8,128)(2,1)S(1)}, f32[3,512,256]{2,1,0:T(8,128)S(1)}) custom-call(bf16[512,256]{1,0:T(8,128)(2,1)S(1)} %get-tuple-element.25.q_ref, bf16[512,256]{1,0:T(8,128)(2,1)S(1)} %get-tuple-element.26.k_ref, ...), custom_call_target="tpu_custom_call" | custom-call | tf_op jit(solution)/shard_map/local/pallas_call | solution.py:435
  12.0 1.2 %collective-permute-done.5.six_ref = bf16[2,32,256]{2,1,0:T(8,128)(2,1)S(1)} collective-permute-done((bf16[2,32,256]{2,1,0:T(8,128)(2,1)S(1)}, bf16[2,32,256]{2,1,0:T(8,128)(2,1)S(1)}, u32[]{:S(2)}, u32[]{:S(2)}) %collective-permute-start.5) | collective-permute-done | bytes 32800 | tf_op jit(solution)/shard_map/ppermute | solution.py:372
  13.2 0.9 %collective-permute-start.6 = (bf16[2,64,256]{2,1,0:T(8,128)(2,1)S(1)}, bf16[2,64,256]{2,1,0:T(8,128)(2,1)S(1)}, u32[]{:S(2)}, u32[]{:S(2)}) collective-permute-start(bf16[2,64,256]{2,1,0:T(8,128)(2,1)S(1)} %join.1.fours_a), channel_id=1, source_target_pairs={{0,4},{4,0},{8,12},{12,8},{16,20},{20,16},{24,28},{28,24},{1,5},{5... | collective-permute-start | bytes 196616 | tf_op jit(solution)/shard_map/ppermute | solution.py:372
  14.2 0.0 collective-permute-done.2.three_a
  14.2 0.6 %collective-permute-done.3.three_b = bf16[2,64,256]{2,1,0:T(8,128)(2,1)S(1)} collective-permute-done((bf16[2,64,256]{2,1,0:T(8,128)(2,1)S(1)}, bf16[2,64,256]{2,1,0:T(8,128)(2,1)S(1)}, u32[]{:S(2)}, u32[]{:S(2)}) %collective-permute-start.3) | collective-permute-done | bytes 65568 | tf_op jit(solution)/shard_map/ppermute | solution.py:372
  14.8 0.0 collective-permute-done.1.first_ref
  14.8 0.5 %coarse.1 = (f32[3,128,256]{2,1,0:T(8,128)S(1)}, bf16[2,32,256]{2,1,0:T(8,128)(2,1)S(1)}) custom-call(bf16[128,256]{1,0:T(8,128)(2,1)S(1)} %get-tuple-element.33.two_q, bf16[64,256]{1,0:T(8,128)(2,1)S(1)} %get-tuple-element.34.three_q, bf16[2,224,256]{2,1,0:T(8,128)(2,1)S(1)} %collective-permute-done.1.first_ref, ...), custom_call_target="tpu_custom_call" | custom-call | flops 2147483648 | bytes 2097152 | tf_op jit(solution)/shard_map/coarse/pallas_call | solution.py:461
  15.3 0.0 collective-permute-done.4.second_ref
  15.3 0.0 copy-start
  15.3 1.0 %mid.1.state = f32[3,512,256]{2,1,0:T(8,128)S(1)} custom-call(bf16[2,128,256]{2,1,0:T(8,128)(2,1)S(1)} %get-tuple-element.32.edge_q, f32[3,128,256]{2,1,0:T(8,128)S(1)} %get-tuple-element.37.coarse, f32[3,512,256]{2,1,0:T(8,128)S(1)} %get-tuple-element.38.state, ...), custom_call_target="tpu_custom_call", output_to_operand_aliasing={{}: (2, {})} | custom-call | tf_op jit(solution)/shard_map/mid/pallas_call | solution.py:477
  16.3 1.1 %collective-permute-done.6.fours_b = bf16[2,64,256]{2,1,0:T(8,128)(2,1)S(1)} collective-permute-done((bf16[2,64,256]{2,1,0:T(8,128)(2,1)S(1)}, bf16[2,64,256]{2,1,0:T(8,128)(2,1)S(1)}, u32[]{:S(2)}, u32[]{:S(2)}) %collective-permute-start.6) | collective-permute-done | bytes 65568 | tf_op jit(solution)/shard_map/ppermute | solution.py:372
  17.5 0.6 %finish.1 = (bf16[128,256]{1,0:T(8,128)(2,1)S(1)}, bf16[128,256]{1,0:T(8,128)(2,1)S(1)}, bf16[128,256]{1,0:T(8,128)(2,1)S(1)}, bf16[128,256]{1,0:T(8,128)(2,1)S(1)}) custom-call(bf16[32,256]{1,0:T(8,128)(2,1)S(1)} %get-tuple-element.31.query_ref.four_q, f32[3,512,256]{2,1,0:T(8,128)S(1)} %mid.1.state, bf16[2,32,256]{2,1,0:T(8,128)(2,1)S(1)} %get-tuple-element.30.four_ref, ...), custom_call_target="tpu_custom_call" | custom-call | tf_op jit(solution)/shard_map/finish/pallas_call | solution.py:497
  18.1 0.1 collective-permute-start.7
  18.2 1.6 %collective-permute-start.8 = (bf16[128,256]{1,0:T(8,128)(2,1)S(1)}, bf16[128,256]{1,0:T(8,128)(2,1)S(1)}, u32[]{:S(2)}, u32[]{:S(2)}) collective-permute-start(bf16[128,256]{1,0:T(8,128)(2,1)S(1)} %get-tuple-element.43), channel_id=1, source_target_pairs={{0,2},{1,3},{2,0},{3,1},{4,6},{5,7},{6,4},{7,5},{8,10},{9,11},{10,... | collective-permute-start | bytes 196616 | tf_op jit(solution)/shard_map/ppermute | solution.py:372
  19.7 0.3 %collective-permute-start.9 = (bf16[128,256]{1,0:T(8,128)(2,1)S(1)}, bf16[128,256]{1,0:T(8,128)(2,1)S(1)}, u32[]{:S(2)}, u32[]{:S(2)}) collective-permute-start(bf16[128,256]{1,0:T(8,128)(2,1)S(1)} %get-tuple-element.44), channel_id=1, source_target_pairs={{0,3},{1,2},{2,1},{3,0},{4,7},{5,6},{6,5},{7,4},{8,11},{9,10},{10,... | collective-permute-start | bytes 196616 | tf_op jit(solution)/shard_map/ppermute | solution.py:372
  20.0 0.0 collective-permute-done.7.next_ref
  20.0 0.0 copy-done
  20.0 0.3 %partial.1.partial_ref = f32[128,1024]{1,0:T(8,128)S(1)} custom-call(bf16[128,256]{1,0:T(8,128)(2,1)S(1)} %get-tuple-element.41.near_ref, bf16[128,256]{1,0:T(8,128)(2,1)S(1)} %collective-permute-done.7.next_ref, bf16[1024,1024]{1,0:T(8,128)(2,1)S(1)} %copy-done), custom_call_target="tpu_custom_call" | custom-call | tf_op jit(solution)/shard_map/partial/pallas_call | solution.py:510
  20.3 2.3 %collective-permute-done.8.refs_0_ = bf16[128,256]{1,0:T(8,128)(2,1)S(1)} collective-permute-done((bf16[128,256]{1,0:T(8,128)(2,1)S(1)}, bf16[128,256]{1,0:T(8,128)(2,1)S(1)}, u32[]{:S(2)}, u32[]{:S(2)}) %collective-permute-start.8) | collective-permute-done | bytes 65568 | tf_op jit(solution)/shard_map/ppermute | solution.py:372
  22.7 1.1 %collective-permute-done.9.refs_1_ = bf16[128,256]{1,0:T(8,128)(2,1)S(1)} collective-permute-done((bf16[128,256]{1,0:T(8,128)(2,1)S(1)}, bf16[128,256]{1,0:T(8,128)(2,1)S(1)}, u32[]{:S(2)}, u32[]{:S(2)}) %collective-permute-start.9) | collective-permute-done | bytes 65568 | tf_op jit(solution)/shard_map/ppermute | solution.py:372
  23.8 1.0 %project.1 = bf16[128,1024]{1,0:T(8,128)(2,1)} custom-call(f32[128,1024]{1,0:T(8,128)S(1)} %partial.1.partial_ref, bf16[128,256]{1,0:T(8,128)(2,1)S(1)} %collective-permute-done.8.refs_0_, bf16[128,256]{1,0:T(8,128)(2,1)S(1)} %collective-permute-done.9.refs_1_, bf16[1024,1024]{1,0:T(8,128)(2,1)S(1)} %copy-done), custom_call_target="tpu_custom_call" | custom-call | tf_op jit(solution)/shard_map/project/pallas_call | solution.py:517
  (2 shorter events, 0.0 us)
Async XLA Ops:
  1.4 13.3 %collective-permute-start.1 = (bf16[2,224,256]{2,1,0:T(8,128)(2,1)S(1)}, bf16[2,224,256]{2,1,0:T(8,128)(2,1)S(1)}, u32[]{:S(2)}, u32[]{:S(2)}) collective-permute-start(bf16[2,224,256]{2,1,0:T(8,128)(2,1)S(1)} %get-tuple-element.35), channel_id=1, source_target_pairs={{0,4},{4,0},{8,12},{12,8},{16,20},{20,16},{24,28},{28,24},{1,5},{5... | collective-permute-start | bytes 688136 | tf_op jit(solution)/shard_map/ppermute | solution.py:372
  4.5 6.0 %collective-permute-start = (bf16[2,32,256]{2,1,0:T(8,128)(2,1)S(1)}, bf16[2,32,256]{2,1,0:T(8,128)(2,1)S(1)}, u32[]{:S(2)}, u32[]{:S(2)}) collective-permute-start(bf16[2,32,256]{2,1,0:T(8,128)(2,1)S(1)} %get-tuple-element.30.four_ref), channel_id=1, source_target_pairs={{0,16},{4,20},{8,24},{12,28},{16,0},{20,4},{24,8},{28,12},{1,17},{... | collective-permute-start | bytes 98312 | tf_op jit(solution)/shard_map/ppermute | solution.py:372
  7.2 6.1 %collective-permute-start.5 = (bf16[2,32,256]{2,1,0:T(8,128)(2,1)S(1)}, bf16[2,32,256]{2,1,0:T(8,128)(2,1)S(1)}, u32[]{:S(2)}, u32[]{:S(2)}) collective-permute-start(bf16[2,32,256]{2,1,0:T(8,128)(2,1)S(1)} %get-tuple-element.30.four_ref), channel_id=1, source_target_pairs={{0,24},{4,28},{8,16},{12,20},{16,8},{20,12},{24,0},{28,4},{1,25},{... | collective-permute-start | bytes 98312 | tf_op jit(solution)/shard_map/ppermute | solution.py:372
  8.5 5.7 %collective-permute-start.2 = (bf16[2,64,256]{2,1,0:T(8,128)(2,1)S(1)}, bf16[2,64,256]{2,1,0:T(8,128)(2,1)S(1)}, u32[]{:S(2)}, u32[]{:S(2)}) collective-permute-start(bf16[2,64,256]{2,1,0:T(8,128)(2,1)S(1)} %get-tuple-element.36), channel_id=1, source_target_pairs={{0,12},{4,8},{8,4},{12,0},{16,28},{20,24},{24,20},{28,16},{1,13},{... | collective-permute-start | bytes 196616 | tf_op jit(solution)/shard_map/ppermute | solution.py:372
  8.7 6.1 %collective-permute-start.3 = (bf16[2,64,256]{2,1,0:T(8,128)(2,1)S(1)}, bf16[2,64,256]{2,1,0:T(8,128)(2,1)S(1)}, u32[]{:S(2)}, u32[]{:S(2)}) collective-permute-start(bf16[2,64,256]{2,1,0:T(8,128)(2,1)S(1)} %get-tuple-element.36), channel_id=1, source_target_pairs={{0,8},{4,12},{8,0},{12,4},{16,24},{20,28},{24,16},{28,20},{1,9},{5... | collective-permute-start | bytes 196616 | tf_op jit(solution)/shard_map/ppermute | solution.py:372
  10.5 4.8 %collective-permute-start.4 = (bf16[2,128,256]{2,1,0:T(8,128)(2,1)S(1)}, bf16[2,128,256]{2,1,0:T(8,128)(2,1)S(1)}, u32[]{:S(2)}, u32[]{:S(2)}) collective-permute-start(bf16[2,128,256]{2,1,0:T(8,128)(2,1)S(1)} %get-tuple-element.39), channel_id=1, source_target_pairs={{0,1},{1,0},{2,3},{3,2},{4,8},{5,9},{6,10},{7,11},{8,4},{9,5},{10,... | collective-permute-start | bytes 393224 | tf_op jit(solution)/shard_map/ppermute | solution.py:383
  13.2 4.3 %collective-permute-start.6 = (bf16[2,64,256]{2,1,0:T(8,128)(2,1)S(1)}, bf16[2,64,256]{2,1,0:T(8,128)(2,1)S(1)}, u32[]{:S(2)}, u32[]{:S(2)}) collective-permute-start(bf16[2,64,256]{2,1,0:T(8,128)(2,1)S(1)} %join.1.fours_a), channel_id=1, source_target_pairs={{0,4},{4,0},{8,12},{12,8},{16,20},{20,16},{24,28},{28,24},{1,5},{5... | collective-permute-start | bytes 196616 | tf_op jit(solution)/shard_map/ppermute | solution.py:372
  15.3 4.7 %copy-start = (bf16[1024,1024]{1,0:T(8,128)(2,1)S(1)}, bf16[1024,1024]{1,0:T(8,128)(2,1)}, u32[]{:S(2)}) copy-start(bf16[1024,1024]{1,0:T(8,128)(2,1)} %refs_2_.1) | copy-start | bytes 6291460
  18.1 1.9 %collective-permute-start.7 = (bf16[128,256]{1,0:T(8,128)(2,1)S(1)}, bf16[128,256]{1,0:T(8,128)(2,1)S(1)}, u32[]{:S(2)}, u32[]{:S(2)}) collective-permute-start(bf16[128,256]{1,0:T(8,128)(2,1)S(1)} %get-tuple-element.42), channel_id=1, source_target_pairs={{0,1},{1,0},{2,3},{3,2},{4,5},{5,4},{6,7},{7,6},{8,9},{9,8},{10,11... | collective-permute-start | bytes 196616 | tf_op jit(solution)/shard_map/ppermute | solution.py:372
  18.2 4.5 %collective-permute-start.8 = (bf16[128,256]{1,0:T(8,128)(2,1)S(1)}, bf16[128,256]{1,0:T(8,128)(2,1)S(1)}, u32[]{:S(2)}, u32[]{:S(2)}) collective-permute-start(bf16[128,256]{1,0:T(8,128)(2,1)S(1)} %get-tuple-element.43), channel_id=1, source_target_pairs={{0,2},{1,3},{2,0},{3,1},{4,6},{5,7},{6,4},{7,5},{8,10},{9,11},{10,... | collective-permute-start | bytes 196616 | tf_op jit(solution)/shard_map/ppermute | solution.py:372
  19.7 4.0 %collective-permute-start.9 = (bf16[128,256]{1,0:T(8,128)(2,1)S(1)}, bf16[128,256]{1,0:T(8,128)(2,1)S(1)}, u32[]{:S(2)}, u32[]{:S(2)}) collective-permute-start(bf16[128,256]{1,0:T(8,128)(2,1)S(1)} %get-tuple-element.44), channel_id=1, source_target_pairs={{0,3},{1,2},{2,1},{3,0},{4,7},{5,6},{6,5},{7,4},{8,11},{9,10},{10,... | collective-permute-start | bytes 196616 | tf_op jit(solution)/shard_map/ppermute | solution.py:372
where the time goes:
time: 25 us; the launch traced here: 24.8 us
  starting transfers between devices  11.9 us (48%)
  Pallas kernels  6.47 us (26%)
  waiting for transfers between devices  6.38 us (26%)
    ppermute x9, starting transfers between devices, swapped(): lax.ppermute(block, axis, [(i, i ^ mask) for i in range(lax.axis_size(axi...  11.9 us
    ppermute x9, waiting for transfers between devices, swapped(): lax.ppermute(block, axis, [(i, i ^ mask) for i in range(lax.axis_size(axi...  6.37 us
    pallas_call x1, Pallas kernels, per_device(): pl.pallas_call(local_kernel, out_shape=[bf16(2, BLOCK, features), bf16(ro...  1.54 us
    pallas_call x1, Pallas kernels, per_device(): pl.pallas_call(pool_kernel, in_specs=[hbm] * 3, out_shape=[bf16(rows, fea...  1.42 us
    pallas_call x1, Pallas kernels, per_device(): pl.pallas_call(project_kernel, in_specs=[vmem] * len(parts), out_specs=hb...  1.04 us
    pallas_call x1, Pallas kernels, per_device(): pl.pallas_call(mid_kernel, out_shape=jax.ShapeDtypeStruct((3, rows, featu...  1.03 us
    pallas_call x1, Pallas kernels, per_device(): pl.pallas_call(finish_kernel, out_shape=[bf16(BLOCK, features) for _ in r...  0.58 us
    pallas_call x1, Pallas kernels, per_device(): pl.pallas_call(coarse_kernel, out_shape=[jax.ShapeDtypeStruct((3, rows //...  0.5 us
  transfers between devices with their start and end apart: 10, of which 5 were waited for; matrix products, arithmetic and copies ran while one was open for 0% of the time, Pallas kernels for 14%

commit v1 on v0

--- a/solution.py
+++ b/solution.py
@@ -13,7 +13,10 @@
 
 neg_fill = -1e30
 root_half = 0.7071067811865476
-log2_scale = HD**-0.5 * 1.4426950408889634
+log2_e = 1.4426950408889634
+log2_scale = HD**-0.5 * log2_e
+least_share = 2.0**-100
+CORES = 2
 
 FAN = 2**LEVELS
 
@@ -233,7 +236,9 @@
             coarse[index, :, pl.ds(pair * PAIR, PAIR)] = field
 
 
-def mid_kernel(edge_q, coarse, state, first_ref, second_ref, out, holds):
+def mid_kernel(edge_q, coarse, state, first_ref, second_ref, fine, *refs):
+    outs, (ready, holds) = refs[:-2], refs[-2:]
+    own = lax.axis_index("head")
     rows = state.shape[1]
     blocks = rows // BLOCK
     position = lax.axis_index("seq")
@@ -267,18 +272,30 @@
             for side, edge in enumerate((0, blocks - 1)):
                 if block == edge:
                     done = merged(done, weigh(holds.at[pair, side], *steps[pair, side]))
-            for index, field in enumerate(done):
-                out[index, here, lanes] = field
+            result = done[1] / done[2]
+            fine[0, here, lanes] = result
+            fine[1, here, lanes] = done[0] + jnp.log(done[2]) * log2_e
+            ready[block, :, lanes] = result.astype(jnp.bfloat16)
+    for step, out in enumerate(outs, CORES):
+        out[...] = ready[own ^ step]
+
+
+def repeated(field):
+    return jnp.concatenate([field] * FAN, axis=0)
+
+
+def share(ahead, behind):
+    return 1.0 / (1.0 + jnp.exp2(behind - ahead))
 
 
 def finish_kernel(
-    four_q, state, four_ref, near_ref, three_a, three_b, fours_a, fours_b, *refs
+    four_q, fine, four_ref, near_ref, three_a, three_b, fours_a, fours_b, *refs
 ):
-    far, refs = refs[:-6], refs[-6:]
-    outs, (attended, four_hold) = refs[:-2], refs[-2:]
-    rows = state.shape[1]
-    blocks = rows // BLOCK
+    refs, (coarse, four_hold) = refs[:-2], refs[-2:]
+    heads = lax.axis_size("head")
+    far, outs = refs[:-heads], refs[-heads:]
     own = lax.axis_index("head")
+    features = four_q.shape[1]
     pairs = four_q.shape[1] // PAIR
     steps = {}
     for pair in range(pairs):
@@ -306,19 +323,64 @@
         )
     for pair in range(pairs):
         lanes = pl.ds(pair * PAIR, PAIR)
-        four = weigh(four_hold.at[pair], *steps[pair])
-        for block in range(blocks):
-            here = slice(block * BLOCK, (block + 1) * BLOCK)
-            coarse = [x[block * SLAB : (block + 1) * SLAB] for x in four]
-            for _ in range(LEVELS):
-                coarse = [doubled(x) for x in coarse]
-            _, numer, rowsum = merged([state[index, here, lanes] for index in range(3)], coarse)
-            attended[block, :, lanes] = (numer / rowsum).astype(jnp.bfloat16)
+        top, numer, rowsum = weigh(four_hold.at[pair], *steps[pair])
+        coarse[0, :, lanes] = numer / rowsum
+        coarse[1, :, lanes] = top + jnp.log(rowsum) * log2_e
     for step, out in enumerate(outs):
-        out[...] = attended[own ^ step]
-
-
-def partial_kernel(near_ref, next_ref, weight_ref, out_ref):
+        block = own ^ step
+        here = pl.ds(pl.multiple_of(block * BLOCK, BLOCK), BLOCK)
+        few = pl.ds(pl.multiple_of(block * SLAB, SLAB), SLAB)
+        shares = []
+        for pair in range(pairs):
+            lanes = pl.ds(pair * PAIR, PAIR)
+            fine_sum, coarse_sum = fine[1, here, lanes], repeated(coarse[1, few, lanes])
+            keep, join = share(fine_sum, coarse_sum), share(coarse_sum, fine_sum)
+            if step < CORES:
+                result = keep * fine[0, here, lanes] + join * repeated(coarse[0, few, lanes])
+                out[:, lanes] = result.astype(jnp.bfloat16)
+            else:
+                signed = jnp.where(fine_sum <= coarse_sum, keep, -jnp.maximum(join, least_share))
+                shares.append(signed.astype(jnp.bfloat16))
+        if step >= CORES:
+            pick = lax.broadcasted_iota(jnp.int32, (2 * SLAB, features), 1) == HD * (
+                lax.broadcasted_iota(jnp.int32, (2 * SLAB, features), 0)
+            )
+            by_head = lax.dot_general(
+                pick.astype(jnp.bfloat16),
+                jnp.concatenate(shares, axis=1),
+                (((1,), (1,)), ((), ())),
+                preferred_element_type=jnp.float32,
+            )[:SLAB]
+            blank = jnp.zeros((SLAB, features - BLOCK), jnp.float32)
+            out[...] = jnp.concatenate(
+                [coarse[0, few, :], jnp.concatenate([by_head, blank], axis=1)], axis=0
+            ).astype(jnp.bfloat16)
+
+
+def joined_parts(early, late_ref):
+    features = early.shape[1]
+    late = late_ref[...].astype(jnp.float32)
+    spread = lax.broadcasted_iota(jnp.int32, (SLAB, features), 1) // HD == (
+        lax.broadcasted_iota(jnp.int32, (SLAB, features), 0)
+    )
+    signed = lax.dot_general(
+        late[SLAB:, :BLOCK].astype(jnp.bfloat16),
+        spread.astype(jnp.bfloat16),
+        (((0,), (0,)), ((), ())),
+        preferred_element_type=jnp.float32,
+    )
+    keep = jnp.where(signed >= 0, signed, 1.0 + signed)
+    join = jnp.where(signed >= 0, 1.0 - signed, -signed)
+    result = keep * early + join * repeated(late[:SLAB])
+    return result.astype(jnp.bfloat16)
+
+
+def stack_kernel(*refs):
+    for index, ref in enumerate(refs[:-1]):
+        refs[-1][index] = ref[...].astype(jnp.float32)
+
+
+def partial_kernel(near_ref, next_ref, early_ref, weight_ref, out_ref):
     own = lax.axis_index("head")
     features = near_ref.shape[1]
     total = None
@@ -331,19 +393,20 @@
     out_ref[...] = total
 
 
-def project_kernel(partial_ref, *refs):
-    parts, (weight_ref, out_hbm, scratch, staged, sems) = refs[:-5], refs[-5:]
+def project_kernel(partial_ref, early_ref, *refs):
+    refs, (weight_ref, out_hbm, scratch, staged, sems) = refs[:-5], refs[-5:]
     own = lax.axis_index("head")
+    parts = [joined_parts(early_ref[index], late) for index, late in enumerate(refs)]
     features = parts[0].shape[1]
     chunk = staged.shape[2]
     copies = []
     for index in range(staged.shape[0]):
         columns = pl.ds(index * chunk, chunk)
         total = partial_ref[:, columns]
-        for step, part in enumerate(parts, 2):
+        for step, part in enumerate(parts, CORES):
             start = pl.multiple_of((own ^ step) * features, features)
             total += jnp.dot(
-                part[...],
+                part,
                 weight_ref[pl.ds(start, features), columns],
                 preferred_element_type=jnp.float32,
             )
@@ -474,14 +537,19 @@
         cost_estimate=pl.CostEstimate(flops=2**31, bytes_accessed=2**21, transcendentals=0),
         name="coarse",
     )(two_q, three_q, first_in, *threes_in)
-    state = pl.pallas_call(
+    away = range(CORES, head_count)
+    fine, *early = pl.pallas_call(
         mid_kernel,
-        out_shape=jax.ShapeDtypeStruct((3, rows, features), jnp.float32),
-        input_output_aliases={2: 0},
-        scratch_shapes=[pltpu.VMEM((pairs, 2, 2 * BLOCK, BLOCK), jnp.float32)],
+        out_shape=[jax.ShapeDtypeStruct((2, rows, features), jnp.float32)]
+        + [bf16(BLOCK, features) for _ in away],
+        scratch_shapes=[
+            pltpu.VMEM((rows // BLOCK, BLOCK, features), jnp.bfloat16),
+            pltpu.VMEM((pairs, 2, 2 * BLOCK, BLOCK), jnp.float32),
+        ],
         compiler_params=params,
         name="mid",
     )(edge_q, coarse, state, first_in, second_in)
+    early_in = [swapped(part, "head", step) for step, part in zip(away, early)]
 
     far = []
     known = 8
@@ -494,29 +562,37 @@
             group = jnp.concatenate([group, fresh], axis=1)
             known *= 2
 
+    near_parts = [bf16(BLOCK, features) for _ in range(CORES)]
     outs = pl.pallas_call(
         finish_kernel,
-        out_shape=[bf16(BLOCK, features) for _ in range(head_count)],
+        out_shape=near_parts + [bf16(2 * SLAB, features) for _ in away],
         scratch_shapes=[
-            pltpu.VMEM((rows // BLOCK, BLOCK, features), jnp.bfloat16),
+            pltpu.VMEM((2, rows // 16, features), jnp.float32),
             pltpu.VMEM((pairs, rows // 8, rows // 16 * seq_count), jnp.float32),
         ],
         compiler_params=params,
         name="finish",
-    )(four_q, state, four, near, *threes_in, fours, fours_in, *far)
-
-    parts = [part if step == 0 else swapped(part, "head", step) for step, part in enumerate(outs)]
+    )(four_q, fine, four, near, *threes_in, fours, fours_in, *far)
+    parts = [outs[0], swapped(outs[1], "head", 1)]
+    late_in = [swapped(part, "head", step) for step, part in zip(away, outs[CORES:])]
     width = out_weight.shape[1]
+    early = pl.pallas_call(
+        stack_kernel,
+        out_shape=jax.ShapeDtypeStruct((len(early_in), BLOCK, features), jnp.float32),
+        compiler_params=params,
+        cost_estimate=pl.CostEstimate(flops=2**32, bytes_accessed=2**20, transcendentals=0),
+        name="stack",
+    )(*early_in)
     partial = pl.pallas_call(
         partial_kernel,
         out_shape=jax.ShapeDtypeStruct((BLOCK, width), jnp.float32),
         compiler_params=params,
         name="partial",
-    )(*parts[:2], out_weight)
+    )(*parts, early, out_weight)
     chunk = 2 * PAIR
     result = pl.pallas_call(
         project_kernel,
-        in_specs=[vmem] * len(parts),
+        in_specs=[vmem] * (3 + len(late_in)),
         out_specs=hbm,
         out_shape=bf16(BLOCK, width),
         scratch_shapes=[
@@ -526,7 +602,7 @@
         ],
         compiler_params=params,
         name="project",
-    )(partial, *parts[2:], out_weight)
+    )(partial, early, *late_in, out_weight)
     return result[None]
 
 

time: 25 us -> 25.3 us (1.012)
  waiting for transfers between devices: 6.38 us -> 4.22 us
  starting transfers between devices: 11.9 us -> 13.7 us
  Pallas kernels: 6.47 us -> 6.8 us
  local copies, waits for them, and re-layouts: 0.01 us -> 0.34 us
    ppermute x9 -> x11, waiting for transfers between devices: 6.37 us -> 4.21 us  [swapped(): lax.ppermute(block, axis, [(i, i ^ mask) for i in range(lax.axis_size(axi...]
    ppermute x9 -> x11, starting transfers between devices: 11.9 us -> 13.7 us  [swapped(): lax.ppermute(block, axis, [(i, i ^ mask) for i in range(lax.axis_size(axi...]
    unnamed x2, local copies, waits for them, and re-layouts: 0.01 us -> 0.34 us
    pallas_call x3 -> x4, Pallas kernels: 2.65 us -> 2.98 us  [the longest x1 1.23 us: per_device(): pl.pallas_call(project_kernel, in_specs=[vmem] * (3 + len(late_in)), out_...]
  transfers between devices with their start and end apart: 10 -> 12, of which waited for: 5 -> 5; matrix products, arithmetic and copies ran while one was open for 0% -> 0% of each run, Pallas kernels for 14% -> 17%
where the time goes in v1:
time: 25.3 us; the launch traced here: 25.1 us
  starting transfers between devices  13.7 us (54%)
  Pallas kernels  6.8 us (27%)
  waiting for transfers between devices  4.22 us (17%)
  local copies, waits for them, and re-layouts  0.34 us (1%)
    ppermute x11, starting transfers between devices, swapped(): lax.ppermute(block, axis, [(i, i ^ mask) for i in range(lax.axis_size(axi...  13.7 us
    ppermute x11, waiting for transfers between devices, swapped(): lax.ppermute(block, axis, [(i, i ^ mask) for i in range(lax.axis_size(axi...  4.21 us
    pallas_call x1, Pallas kernels, per_device(): pl.pallas_call(local_kernel, out_shape=[bf16(2, BLOCK, features), bf16(ro...  1.54 us
    pallas_call x1, Pallas kernels, per_device(): pl.pallas_call(pool_kernel, in_specs=[hbm] * 3, out_shape=[bf16(rows, fea...  1.42 us
    pallas_call x1, Pallas kernels, per_device(): pl.pallas_call(project_kernel, in_specs=[vmem] * (3 + len(late_in)), out_...  1.23 us
    pallas_call x1, Pallas kernels, per_device(): pl.pallas_call(mid_kernel, out_shape=[jax.ShapeDtypeStruct((2, rows, feat...  0.93 us
    pallas_call x1, Pallas kernels, per_device(): pl.pallas_call(finish_kernel, out_shape=near_parts + [bf16(2 * SLAB, feat...  0.8 us
  transfers between devices with their start and end apart: 12, of which 5 were waited for; matrix products, arithmetic and copies ran while one was open for 0% of the time, Pallas kernels for 17%

profile of v1, /device:TPU:0, one launch (start us, length us, event | category | flops | bytes accessed | tf_op | source)
XLA Modules:
  0.0 25.1 jit_solution(5361098410197546457)
XLA Ops:
  0.0 1.4 %pool.1 = (bf16[512,256]{1,0:T(8,128)(2,1)S(1)}, bf16[512,256]{1,0:T(8,128)(2,1)S(1)}, bf16[512,256]{1,0:T(8,128)(2,1)S(1)}, bf16[2,224,256]{2,1,0:T(8,128)(2,1)...) custom-call(bf16[1,512,256]{2,1,0:T(8,128)(2,1)} %k_hbm.1, bf16[1,512,256]{2,1,0:T(8,128)(2,1)} %v_hbm.1, ...), custom_call_target="tpu_custom_call" | custom-call | tf_op jit(solution)/shard_map/pool/pallas_call | solution.py:462
  1.4 3.0 %collective-permute-start.1 = (bf16[2,224,256]{2,1,0:T(8,128)(2,1)S(1)}, bf16[2,224,256]{2,1,0:T(8,128)(2,1)S(1)}, u32[]{:S(2)}, u32[]{:S(2)}) collective-permute-start(bf16[2,224,256]{2,1,0:T(8,128)(2,1)S(1)} %get-tuple-element.38), channel_id=1, source_target_pairs={{0,4},{4,0},{8,12},{12,8},{16,20},{20,16},{24,28},{28,24},{1,5},{5... | collective-permute-start | bytes 688136 | tf_op jit(solution)/shard_map/ppermute | solution.py:435
  4.5 2.7 %collective-permute-start = (bf16[2,32,256]{2,1,0:T(8,128)(2,1)S(1)}, bf16[2,32,256]{2,1,0:T(8,128)(2,1)S(1)}, u32[]{:S(2)}, u32[]{:S(2)}) collective-permute-start(bf16[2,32,256]{2,1,0:T(8,128)(2,1)S(1)} %get-tuple-element.33.four_ref), channel_id=1, source_target_pairs={{0,16},{4,20},{8,24},{12,28},{16,0},{20,4},{24,8},{28,12},{1,17},{... | collective-permute-start | bytes 98312 | tf_op jit(solution)/shard_map/ppermute | solution.py:435
  7.2 1.3 %collective-permute-start.5 = (bf16[2,32,256]{2,1,0:T(8,128)(2,1)S(1)}, bf16[2,32,256]{2,1,0:T(8,128)(2,1)S(1)}, u32[]{:S(2)}, u32[]{:S(2)}) collective-permute-start(bf16[2,32,256]{2,1,0:T(8,128)(2,1)S(1)} %get-tuple-element.33.four_ref), channel_id=1, source_target_pairs={{0,24},{4,28},{8,16},{12,20},{16,8},{20,12},{24,0},{28,4},{1,25},{... | collective-permute-start | bytes 98312 | tf_op jit(solution)/shard_map/ppermute | solution.py:435
  8.5 0.2 collective-permute-start.2
  8.7 1.8 %collective-permute-start.3 = (bf16[2,64,256]{2,1,0:T(8,128)(2,1)S(1)}, bf16[2,64,256]{2,1,0:T(8,128)(2,1)S(1)}, u32[]{:S(2)}, u32[]{:S(2)}) collective-permute-start(bf16[2,64,256]{2,1,0:T(8,128)(2,1)S(1)} %get-tuple-element.39), channel_id=1, source_target_pairs={{0,8},{4,12},{8,0},{12,4},{16,24},{20,28},{24,16},{28,20},{1,9},{5... | collective-permute-start | bytes 196616 | tf_op jit(solution)/shard_map/ppermute | solution.py:435
  10.5 0.0 collective-permute-done.four_ref
  10.5 0.0 collective-permute-start.4
  10.5 1.5 %local.1 = (bf16[2,128,256]{2,1,0:T(8,128)(2,1)S(1)}, bf16[128,256]{1,0:T(8,128)(2,1)S(1)}, bf16[64,256]{1,0:T(8,128)(2,1)S(1)}, bf16[32,256]{1,0:T(8,128)(2,1)S(1)}, f32[3,512,256]{2,1,0:T(8,128)S(1)}) custom-call(bf16[512,256]{1,0:T(8,128)(2,1)S(1)} %get-tuple-element.28.q_ref, bf16[512,256]{1,0:T(8,128)(2,1)S(1)} %get-tuple-element.29.k_ref, ...), custom_call_target="tpu_custom_call" | custom-call | tf_op jit(solution)/shard_map/local/pallas_call | solution.py:498
  12.0 1.2 %collective-permute-done.5.six_ref = bf16[2,32,256]{2,1,0:T(8,128)(2,1)S(1)} collective-permute-done((bf16[2,32,256]{2,1,0:T(8,128)(2,1)S(1)}, bf16[2,32,256]{2,1,0:T(8,128)(2,1)S(1)}, u32[]{:S(2)}, u32[]{:S(2)}) %collective-permute-start.5) | collective-permute-done | bytes 32800 | tf_op jit(solution)/shard_map/ppermute | solution.py:435
  13.2 0.9 %collective-permute-start.6 = (bf16[2,64,256]{2,1,0:T(8,128)(2,1)S(1)}, bf16[2,64,256]{2,1,0:T(8,128)(2,1)S(1)}, u32[]{:S(2)}, u32[]{:S(2)}) collective-permute-start(bf16[2,64,256]{2,1,0:T(8,128)(2,1)S(1)} %join.1.fours_a), channel_id=1, source_target_pairs={{0,4},{4,0},{8,12},{12,8},{16,20},{20,16},{24,28},{28,24},{1,5},{5... | collective-permute-start | bytes 196616 | tf_op jit(solution)/shard_map/ppermute | solution.py:435
  14.2 0.0 collective-permute-done.2.three_a
  14.2 0.6 %collective-permute-done.3.three_b = bf16[2,64,256]{2,1,0:T(8,128)(2,1)S(1)} collective-permute-done((bf16[2,64,256]{2,1,0:T(8,128)(2,1)S(1)}, bf16[2,64,256]{2,1,0:T(8,128)(2,1)S(1)}, u32[]{:S(2)}, u32[]{:S(2)}) %collective-permute-start.3) | collective-permute-done | bytes 65568 | tf_op jit(solution)/shard_map/ppermute | solution.py:435
  14.8 0.0 collective-permute-done.1.first_ref
  14.8 0.5 %coarse.1 = (f32[3,128,256]{2,1,0:T(8,128)S(1)}, bf16[2,32,256]{2,1,0:T(8,128)(2,1)S(1)}) custom-call(bf16[128,256]{1,0:T(8,128)(2,1)S(1)} %get-tuple-element.36.two_q, bf16[64,256]{1,0:T(8,128)(2,1)S(1)} %get-tuple-element.37.three_q, bf16[2,224,256]{2,1,0:T(8,128)(2,1)S(1)} %collective-permute-done.1.first_ref, ...), custom_call_target="tpu_custom_call" | custom-call | flops 2147483648 | bytes 2097152 | tf_op jit(solution)/shard_map/coarse/pallas_call | solution.py:524
  15.3 0.0 collective-permute-done.4.second_ref
  15.3 0.9 %mid.1 = (f32[2,512,256]{2,1,0:T(8,128)S(1)}, bf16[128,256]{1,0:T(8,128)(2,1)S(1)}, bf16[128,256]{1,0:T(8,128)(2,1)S(1)}) custom-call(bf16[2,128,256]{2,1,0:T(8,128)(2,1)S(1)} %get-tuple-element.35.edge_q, f32[3,128,256]{2,1,0:T(8,128)S(1)} %get-tuple-element.40.coarse, f32[3,512,256]{2,1,0:T(8,128)S(1)} %get-tuple-element.41.state, ...), custom_call_target="tpu_custom_call" | custom-call | tf_op jit(solution)/shard_map/mid/pallas_call | solution.py:541
  16.2 1.6 %collective-permute-start.8 = (bf16[128,256]{1,0:T(8,128)(2,1)S(1)}, bf16[128,256]{1,0:T(8,128)(2,1)S(1)}, u32[]{:S(2)}, u32[]{:S(2)}) collective-permute-start(bf16[128,256]{1,0:T(8,128)(2,1)S(1)} %get-tuple-element.47), channel_id=1, source_target_pairs={{0,2},{1,3},{2,0},{3,1},{4,6},{5,7},{6,4},{7,5},{8,10},{9,11},{10,... | collective-permute-start | bytes 196616 | tf_op jit(solution)/shard_map/ppermute | solution.py:435
  17.8 0.0 collective-permute-start.9
  17.8 0.0 collective-permute-done.6.fours_b
  17.8 0.8 %finish.1 = (bf16[128,256]{1,0:T(8,128)(2,1)S(1)}, bf16[128,256]{1,0:T(8,128)(2,1)S(1)}, bf16[16,256]{1,0:T(8,128)(2,1)S(1)}, bf16[16,256]{1,0:T(8,128)(2,1)S(1)}) custom-call(bf16[32,256]{1,0:T(8,128)(2,1)S(1)} %get-tuple-element.34.query_ref.four_q, f32[2,512,256]{2,1,0:T(8,128)S(1)} %get-tuple-element.43.fine, ...), custom_call_target="tpu_custom_call" | custom-call | tf_op jit(solution)/shard_map/finish/pallas_call | solution.py:566
  18.6 0.7 %collective-permute-start.7 = (bf16[128,256]{1,0:T(8,128)(2,1)S(1)}, bf16[128,256]{1,0:T(8,128)(2,1)S(1)}, u32[]{:S(2)}, u32[]{:S(2)}) collective-permute-start(bf16[128,256]{1,0:T(8,128)(2,1)S(1)} %get-tuple-element.46), channel_id=1, source_target_pairs={{0,1},{1,0},{2,3},{3,2},{4,5},{5,4},{6,7},{7,6},{8,9},{9,8},{10,11... | collective-permute-start | bytes 196616 | tf_op jit(solution)/shard_map/ppermute | solution.py:435
  19.3 1.5 %collective-permute-start.10 = (bf16[16,256]{1,0:T(8,128)(2,1)S(1)}, bf16[16,256]{1,0:T(8,128)(2,1)S(1)}, u32[]{:S(2)}, u32[]{:S(2)}) collective-permute-start(bf16[16,256]{1,0:T(8,128)(2,1)S(1)} %get-tuple-element.49), channel_id=1, source_target_pairs={{0,2},{1,3},{2,0},{3,1},{4,6},{5,7},{6,4},{7,5},{8,10},{9,11},{10,... | collective-permute-start | bytes 24584 | tf_op jit(solution)/shard_map/ppermute | solution.py:435
  20.8 0.0 copy-start
  20.8 0.0 collective-permute-start.11
  20.8 0.0 collective-permute-done.8.refs_0_
  20.8 1.2 %collective-permute-done.9.refs_1_ = bf16[128,256]{1,0:T(8,128)(2,1)S(1)} collective-permute-done((bf16[128,256]{1,0:T(8,128)(2,1)S(1)}, bf16[128,256]{1,0:T(8,128)(2,1)S(1)}, u32[]{:S(2)}, u32[]{:S(2)}) %collective-permute-start.9) | collective-permute-done | bytes 65568 | tf_op jit(solution)/shard_map/ppermute | solution.py:435
  22.0 0.0 collective-permute-done.7.next_ref
  22.0 0.3 %copy-done = bf16[1024,1024]{1,0:T(8,128)(2,1)S(1)} copy-done((bf16[1024,1024]{1,0:T(8,128)(2,1)S(1)}, bf16[1024,1024]{1,0:T(8,128)(2,1)}, u32[]{:S(2)}) %copy-start) | copy-done | bytes 2097176
  22.3 0.3 %partial.1.partial_ref = f32[128,1024]{1,0:T(8,128)S(1)} custom-call(bf16[128,256]{1,0:T(8,128)(2,1)S(1)} %get-tuple-element.45.near_ref, bf16[128,256]{1,0:T(8,128)(2,1)S(1)} %collective-permute-done.7.next_ref, f32[2,128,256]{2,1,0:T(8,128)S(1)} %stack.1.early_ref, bf16[1024,1024]{1,0:T(8,128)(2,1)S(1)} %copy-done), custom_call_target="tpu_custom_call" | custom-call | tf_op jit(solution)/shard_map/partial/pallas_call | solution.py:586
  22.7 0.2 collective-permute-done.10.refs_0_
  22.9 0.9 %collective-permute-done.11.refs_1_ = bf16[16,256]{1,0:T(8,128)(2,1)S(1)} collective-permute-done((bf16[16,256]{1,0:T(8,128)(2,1)S(1)}, bf16[16,256]{1,0:T(8,128)(2,1)S(1)}, u32[]{:S(2)}, u32[]{:S(2)}) %collective-permute-start.11) | collective-permute-done | bytes 8224 | tf_op jit(solution)/shard_map/ppermute | solution.py:435
  23.9 1.2 %project.1 = bf16[128,1024]{1,0:T(8,128)(2,1)} custom-call(f32[128,1024]{1,0:T(8,128)S(1)} %partial.1.partial_ref, f32[2,128,256]{2,1,0:T(8,128)S(1)} %stack.1.early_ref, bf16[16,256]{1,0:T(8,128)(2,1)S(1)} %collective-permute-done.10.refs_0_, bf16[16,256]{1,0:T(8,128)(2,1)S(1)} %collective-permute-done.11.refs_1_, bf16[1024,1024]{1,0:T(8,128)(2,1)S(1)} %copy-done), custom_call_target="tpu_custom_call" | custom-call | tf_op jit(solution)/shard_map/project/pallas_call | solution.py:593
  (3 shorter events, 0.1 us)
Async XLA Ops:
  1.4 13.3 %collective-permute-start.1 = (bf16[2,224,256]{2,1,0:T(8,128)(2,1)S(1)}, bf16[2,224,256]{2,1,0:T(8,128)(2,1)S(1)}, u32[]{:S(2)}, u32[]{:S(2)}) collective-permute-start(bf16[2,224,256]{2,1,0:T(8,128)(2,1)S(1)} %get-tuple-element.38), channel_id=1, source_target_pairs={{0,4},{4,0},{8,12},{12,8},{16,20},{20,16},{24,28},{28,24},{1,5},{5... | collective-permute-start | bytes 688136 | tf_op jit(solution)/shard_map/ppermute | solution.py:435
  4.5 6.0 %collective-permute-start = (bf16[2,32,256]{2,1,0:T(8,128)(2,1)S(1)}, bf16[2,32,256]{2,1,0:T(8,128)(2,1)S(1)}, u32[]{:S(2)}, u32[]{:S(2)}) collective-permute-start(bf16[2,32,256]{2,1,0:T(8,128)(2,1)S(1)} %get-tuple-element.33.four_ref), channel_id=1, source_target_pairs={{0,16},{4,20},{8,24},{12,28},{16,0},{20,4},{24,8},{28,12},{1,17},{... | collective-permute-start | bytes 98312 | tf_op jit(solution)/shard_map/ppermute | solution.py:435
  7.2 6.1 %collective-permute-start.5 = (bf16[2,32,256]{2,1,0:T(8,128)(2,1)S(1)}, bf16[2,32,256]{2,1,0:T(8,128)(2,1)S(1)}, u32[]{:S(2)}, u32[]{:S(2)}) collective-permute-start(bf16[2,32,256]{2,1,0:T(8,128)(2,1)S(1)} %get-tuple-element.33.four_ref), channel_id=1, source_target_pairs={{0,24},{4,28},{8,16},{12,20},{16,8},{20,12},{24,0},{28,4},{1,25},{... | collective-permute-start | bytes 98312 | tf_op jit(solution)/shard_map/ppermute | solution.py:435
  8.5 5.7 %collective-permute-start.2 = (bf16[2,64,256]{2,1,0:T(8,128)(2,1)S(1)}, bf16[2,64,256]{2,1,0:T(8,128)(2,1)S(1)}, u32[]{:S(2)}, u32[]{:S(2)}) collective-permute-start(bf16[2,64,256]{2,1,0:T(8,128)(2,1)S(1)} %get-tuple-element.39), channel_id=1, source_target_pairs={{0,12},{4,8},{8,4},{12,0},{16,28},{20,24},{24,20},{28,16},{1,13},{... | collective-permute-start | bytes 196616 | tf_op jit(solution)/shard_map/ppermute | solution.py:435
  8.7 6.1 %collective-permute-start.3 = (bf16[2,64,256]{2,1,0:T(8,128)(2,1)S(1)}, bf16[2,64,256]{2,1,0:T(8,128)(2,1)S(1)}, u32[]{:S(2)}, u32[]{:S(2)}) collective-permute-start(bf16[2,64,256]{2,1,0:T(8,128)(2,1)S(1)} %get-tuple-element.39), channel_id=1, source_target_pairs={{0,8},{4,12},{8,0},{12,4},{16,24},{20,28},{24,16},{28,20},{1,9},{5... | collective-permute-start | bytes 196616 | tf_op jit(solution)/shard_map/ppermute | solution.py:435
  10.5 4.8 %collective-permute-start.4 = (bf16[2,128,256]{2,1,0:T(8,128)(2,1)S(1)}, bf16[2,128,256]{2,1,0:T(8,128)(2,1)S(1)}, u32[]{:S(2)}, u32[]{:S(2)}) collective-permute-start(bf16[2,128,256]{2,1,0:T(8,128)(2,1)S(1)} %get-tuple-element.42), channel_id=1, source_target_pairs={{0,1},{1,0},{2,3},{3,2},{4,8},{5,9},{6,10},{7,11},{8,4},{9,5},{10,... | collective-permute-start | bytes 393224 | tf_op jit(solution)/shard_map/ppermute | solution.py:446
  13.2 4.6 %collective-permute-start.6 = (bf16[2,64,256]{2,1,0:T(8,128)(2,1)S(1)}, bf16[2,64,256]{2,1,0:T(8,128)(2,1)S(1)}, u32[]{:S(2)}, u32[]{:S(2)}) collective-permute-start(bf16[2,64,256]{2,1,0:T(8,128)(2,1)S(1)} %join.1.fours_a), channel_id=1, source_target_pairs={{0,4},{4,0},{8,12},{12,8},{16,20},{20,16},{24,28},{28,24},{1,5},{5... | collective-permute-start | bytes 196616 | tf_op jit(solution)/shard_map/ppermute | solution.py:435
  16.2 4.5 %collective-permute-start.8 = (bf16[128,256]{1,0:T(8,128)(2,1)S(1)}, bf16[128,256]{1,0:T(8,128)(2,1)S(1)}, u32[]{:S(2)}, u32[]{:S(2)}) collective-permute-start(bf16[128,256]{1,0:T(8,128)(2,1)S(1)} %get-tuple-element.47), channel_id=1, source_target_pairs={{0,2},{1,3},{2,0},{3,1},{4,6},{5,7},{6,4},{7,5},{8,10},{9,11},{10,... | collective-permute-start | bytes 196616 | tf_op jit(solution)/shard_map/ppermute | solution.py:435
  17.8 4.2 %collective-permute-start.9 = (bf16[128,256]{1,0:T(8,128)(2,1)S(1)}, bf16[128,256]{1,0:T(8,128)(2,1)S(1)}, u32[]{:S(2)}, u32[]{:S(2)}) collective-permute-start(bf16[128,256]{1,0:T(8,128)(2,1)S(1)} %get-tuple-element.48), channel_id=1, source_target_pairs={{0,3},{1,2},{2,1},{3,0},{4,7},{5,6},{6,5},{7,4},{8,11},{9,10},{10,... | collective-permute-start | bytes 196616 | tf_op jit(solution)/shard_map/ppermute | solution.py:435
  18.6 3.4 %collective-permute-start.7 = (bf16[128,256]{1,0:T(8,128)(2,1)S(1)}, bf16[128,256]{1,0:T(8,128)(2,1)S(1)}, u32[]{:S(2)}, u32[]{:S(2)}) collective-permute-start(bf16[128,256]{1,0:T(8,128)(2,1)S(1)} %get-tuple-element.46), channel_id=1, source_target_pairs={{0,1},{1,0},{2,3},{3,2},{4,5},{5,4},{6,7},{7,6},{8,9},{9,8},{10,11... | collective-permute-start | bytes 196616 | tf_op jit(solution)/shard_map/ppermute | solution.py:435
  19.3 3.7 %collective-permute-start.10 = (bf16[16,256]{1,0:T(8,128)(2,1)S(1)}, bf16[16,256]{1,0:T(8,128)(2,1)S(1)}, u32[]{:S(2)}, u32[]{:S(2)}) collective-permute-start(bf16[16,256]{1,0:T(8,128)(2,1)S(1)} %get-tuple-element.49), channel_id=1, source_target_pairs={{0,2},{1,3},{2,0},{3,1},{4,6},{5,7},{6,4},{7,5},{8,10},{9,11},{10,... | collective-permute-start | bytes 24584 | tf_op jit(solution)/shard_map/ppermute | solution.py:435
  20.8 1.6 %copy-start = (bf16[1024,1024]{1,0:T(8,128)(2,1)S(1)}, bf16[1024,1024]{1,0:T(8,128)(2,1)}, u32[]{:S(2)}) copy-start(bf16[1024,1024]{1,0:T(8,128)(2,1)} %refs_2_.1) | copy-start | bytes 6291460
  20.8 3.1 %collective-permute-start.11 = (bf16[16,256]{1,0:T(8,128)(2,1)S(1)}, bf16[16,256]{1,0:T(8,128)(2,1)S(1)}, u32[]{:S(2)}, u32[]{:S(2)}) collective-permute-start(bf16[16,256]{1,0:T(8,128)(2,1)S(1)} %get-tuple-element.50), channel_id=1, source_target_pairs={{0,3},{1,2},{2,1},{3,0},{4,7},{5,6},{6,5},{7,4},{8,11},{9,10},{10,... | collective-permute-start | bytes 24584 | tf_op jit(solution)/shard_map/ppermute | solution.py:435

commit v2 on v0

--- a/solution.py
+++ b/solution.py
@@ -13,7 +13,8 @@
 
 neg_fill = -1e30
 root_half = 0.7071067811865476
-log2_scale = HD**-0.5 * 1.4426950408889634
+log2_e = 1.4426950408889634
+log2_scale = HD**-0.5 * log2_e
 
 FAN = 2**LEVELS
 
@@ -39,7 +40,7 @@
 
 
 def pool_kernel(
-    k_hbm, v_hbm, q_hbm, k_ref, v_ref, q_ref, first_ref, one_ref, two_ref, scratch, sems, q_sem
+    k_hbm, v_hbm, k_ref, v_ref, first_ref, one_ref, two_ref, scratch, sems
 ):
     rows = k_ref.shape[0]
     blocks = rows // BLOCK
@@ -52,8 +53,6 @@
             )
             copy.start()
             arrivals.append((block, which, target, copy))
-    q_copy = pltpu.make_async_copy(q_hbm.at[0], q_ref, q_sem.at[0])
-    q_copy.start()
     even = lax.rem(lax.axis_index("seq"), 2) == 0
     for block, which, ref, copy in arrivals:
         copy.wait()
@@ -70,7 +69,6 @@
         first_ref[which, BLOCK:, :] = jnp.where(
             even, two_ref[which, :inner, :], two_ref[which, BLOCK // 4 :, :]
         )
-    q_copy.wait()
 
 
 def repooled(field):
@@ -233,7 +231,7 @@
             coarse[index, :, pl.ds(pair * PAIR, PAIR)] = field
 
 
-def mid_kernel(edge_q, coarse, state, first_ref, second_ref, out, holds):
+def mid_kernel(edge_q, coarse, state, first_ref, second_ref, fine, holds):
     rows = state.shape[1]
     blocks = rows // BLOCK
     position = lax.axis_index("seq")
@@ -267,17 +265,20 @@
             for side, edge in enumerate((0, blocks - 1)):
                 if block == edge:
                     done = merged(done, weigh(holds.at[pair, side], *steps[pair, side]))
-            for index, field in enumerate(done):
-                out[index, here, lanes] = field
+            fine[0, here, lanes] = done[1] / done[2]
+            fine[1, here, lanes] = done[0] + jnp.log(done[2]) * log2_e
+
+
+def repeated(field):
+    return jnp.concatenate([field] * FAN, axis=0)
 
 
 def finish_kernel(
-    four_q, state, four_ref, near_ref, three_a, three_b, fours_a, fours_b, *refs
+    four_q, fine, four_ref, near_ref, three_a, three_b, fours_a, fours_b, *refs
 ):
     far, refs = refs[:-6], refs[-6:]
     outs, (attended, four_hold) = refs[:-2], refs[-2:]
-    rows = state.shape[1]
-    blocks = rows // BLOCK
+    blocks = fine.shape[1] // BLOCK
     own = lax.axis_index("head")
     pairs = four_q.shape[1] // PAIR
     steps = {}
@@ -306,29 +307,25 @@
         )
     for pair in range(pairs):
         lanes = pl.ds(pair * PAIR, PAIR)
-        four = weigh(four_hold.at[pair], *steps[pair])
+        top, numer, rowsum = weigh(four_hold.at[pair], *steps[pair])
+        result, log_sum = numer / rowsum, top + jnp.log(rowsum) * log2_e
         for block in range(blocks):
             here = slice(block * BLOCK, (block + 1) * BLOCK)
-            coarse = [x[block * SLAB : (block + 1) * SLAB] for x in four]
-            for _ in range(LEVELS):
-                coarse = [doubled(x) for x in coarse]
-            _, numer, rowsum = merged([state[index, here, lanes] for index in range(3)], coarse)
-            attended[block, :, lanes] = (numer / rowsum).astype(jnp.bfloat16)
+            few = slice(block * SLAB, (block + 1) * SLAB)
+            ours = fine[0, here, lanes]
+            keep = 1.0 / (1.0 + jnp.exp2(repeated(log_sum[few]) - fine[1, here, lanes]))
+            theirs = repeated(result[few])
+            attended[block, :, lanes] = (theirs + keep * (ours - theirs)).astype(jnp.bfloat16)
     for step, out in enumerate(outs):
         out[...] = attended[own ^ step]
 
 
-def partial_kernel(near_ref, next_ref, weight_ref, out_ref):
-    own = lax.axis_index("head")
-    features = near_ref.shape[1]
-    total = None
-    for step, part in enumerate((near_ref, next_ref)):
-        start = pl.multiple_of((own ^ step) * features, features)
-        product = jnp.dot(
-            part[...], weight_ref[pl.ds(start, features), :], preferred_element_type=jnp.float32
-        )
-        total = product if total is None else total + product
-    out_ref[...] = total
+def partial_kernel(own_ref, weight_ref, out_ref):
+    features = own_ref.shape[1]
+    start = pl.multiple_of(lax.axis_index("head") * features, features)
+    out_ref[...] = jnp.dot(
+        own_ref[...], weight_ref[pl.ds(start, features), :], preferred_element_type=jnp.float32
+    )
 
 
 def project_kernel(partial_ref, *refs):
@@ -340,7 +337,7 @@
     for index in range(staged.shape[0]):
         columns = pl.ds(index * chunk, chunk)
         total = partial_ref[:, columns]
-        for step, part in enumerate(parts, 2):
+        for step, part in zip(range(len(parts), 0, -1), parts):
             start = pl.multiple_of((own ^ step) * features, features)
             total += jnp.dot(
                 part[...],
@@ -385,9 +382,8 @@
 
 def per_device(queries, key_vectors, value_vectors, out_weight):
     rows, features = queries.shape[1:]
-    queries, key_vectors, value_vectors = [
-        pltpu.with_memory_space_constraint(x, pltpu.HBM)
-        for x in (queries, key_vectors, value_vectors)
+    key_vectors, value_vectors = [
+        pltpu.with_memory_space_constraint(x, pltpu.HBM) for x in (key_vectors, value_vectors)
     ]
     pairs = features // PAIR
     seq_count, head_count = lax.axis_size("seq"), lax.axis_size("head")
@@ -396,11 +392,10 @@
 
     hbm = pl.BlockSpec(memory_space=pltpu.HBM)
     vmem = pl.BlockSpec(memory_space=pltpu.VMEM)
-    keys, values, ours, first, one, two = pl.pallas_call(
+    keys, values, first, one, two = pl.pallas_call(
         pool_kernel,
-        in_specs=[hbm] * 3,
+        in_specs=[hbm] * 2,
         out_shape=[
-            bf16(rows, features),
             bf16(rows, features),
             bf16(rows, features),
             bf16(2, BLOCK + rows // 4 - BLOCK // 4, features),
@@ -410,11 +405,10 @@
         scratch_shapes=[
             pltpu.VMEM((2, rows // BLOCK, pairs, BLOCK, PAIR), jnp.float32),
             pltpu.SemaphoreType.DMA((2, rows // BLOCK)),
-            pltpu.SemaphoreType.DMA((1,)),
         ],
         compiler_params=params,
         name="pool",
-    )(key_vectors, value_vectors, queries)
+    )(key_vectors, value_vectors)
     second, three, four = pl.pallas_call(
         deeper_kernel,
         out_shape=[
@@ -448,7 +442,7 @@
         ],
         compiler_params=params,
         name="local",
-    )(ours, keys, values, one, four_in)
+    )(queries[0], keys, values, one, four_in)
 
     fours = pl.pallas_call(
         join_kernel,
@@ -474,10 +468,9 @@
         cost_estimate=pl.CostEstimate(flops=2**31, bytes_accessed=2**21, transcendentals=0),
         name="coarse",
     )(two_q, three_q, first_in, *threes_in)
-    state = pl.pallas_call(
+    fine = pl.pallas_call(
         mid_kernel,
-        out_shape=jax.ShapeDtypeStruct((3, rows, features), jnp.float32),
-        input_output_aliases={2: 0},
+        out_shape=jax.ShapeDtypeStruct((2, rows, features), jnp.float32),
         scratch_shapes=[pltpu.VMEM((pairs, 2, 2 * BLOCK, BLOCK), jnp.float32)],
         compiler_params=params,
         name="mid",
@@ -503,20 +496,20 @@
         ],
         compiler_params=params,
         name="finish",
-    )(four_q, state, four, near, *threes_in, fours, fours_in, *far)
-
-    parts = [part if step == 0 else swapped(part, "head", step) for step, part in enumerate(outs)]
+    )(four_q, fine, four, near, *threes_in, fours, fours_in, *far)
+
+    parts = [swapped(outs[step], "head", step) for step in range(head_count - 1, 0, -1)]
     width = out_weight.shape[1]
     partial = pl.pallas_call(
         partial_kernel,
         out_shape=jax.ShapeDtypeStruct((BLOCK, width), jnp.float32),
         compiler_params=params,
         name="partial",
-    )(*parts[:2], out_weight)
+    )(outs[0], out_weight)
     chunk = 2 * PAIR
     result = pl.pallas_call(
         project_kernel,
-        in_specs=[vmem] * len(parts),
+        in_specs=[vmem] * (len(parts) + 2),
         out_specs=hbm,
         out_shape=bf16(BLOCK, width),
         scratch_shapes=[
@@ -526,7 +519,7 @@
         ],
         compiler_params=params,
         name="project",
-    )(partial, *parts[2:], out_weight)
+    )(partial, *parts, out_weight)
     return result[None]
 
 

time: 25 us -> 25.2 us (level)
  waiting for transfers between devices: 6.38 us -> 6.77 us
    ppermute x9, waiting for transfers between devices: 6.37 us -> 6.77 us  [swapped(): lax.ppermute(block, axis, [(i, i ^ mask) for i in range(lax.axis_size(axi...]
  transfers between devices with their start and end apart: 10 -> 10, of which waited for: 5 -> 5; matrix products, arithmetic and copies ran while one was open for 0% -> 0% of each run, Pallas kernels for 14% -> 13%
where the time goes in v2:
time: 25.2 us; the launch traced here: 25.1 us
  starting transfers between devices  11.9 us (47%)
  waiting for transfers between devices  6.77 us (27%)
  Pallas kernels  6.33 us (25%)
    ppermute x9, starting transfers between devices, swapped(): lax.ppermute(block, axis, [(i, i ^ mask) for i in range(lax.axis_size(axi...  11.9 us
    ppermute x9, waiting for transfers between devices, swapped(): lax.ppermute(block, axis, [(i, i ^ mask) for i in range(lax.axis_size(axi...  6.77 us
    pallas_call x1, Pallas kernels, per_device(): pl.pallas_call(local_kernel, out_shape=[bf16(2, BLOCK, features), bf16(ro...  1.54 us
    pallas_call x1, Pallas kernels, per_device(): pl.pallas_call(pool_kernel, in_specs=[hbm] * 2, out_shape=[bf16(rows, fea...  1.41 us
    pallas_call x1, Pallas kernels, per_device(): pl.pallas_call(project_kernel, in_specs=[vmem] * (len(parts) + 2), out_sp...  1.11 us
    pallas_call x1, Pallas kernels, per_device(): pl.pallas_call(mid_kernel, out_shape=jax.ShapeDtypeStruct((2, rows, featu...  0.91 us
    pallas_call x1, Pallas kernels, per_device(): pl.pallas_call(finish_kernel, out_shape=[bf16(BLOCK, features) for _ in r...  0.58 us
  transfers between devices with their start and end apart: 10, of which 5 were waited for; matrix products, arithmetic and copies ran while one was open for 0% of the time, Pallas kernels for 13%

profile of v2, /device:TPU:0, one launch (start us, length us, event | category | flops | bytes accessed | tf_op | source)
XLA Modules:
  0.0 25.1 jit_solution(14541676377013450051)
XLA Ops:
  0.0 1.4 %pool.1 = (bf16[512,256]{1,0:T(8,128)(2,1)S(1)}, bf16[512,256]{1,0:T(8,128)(2,1)S(1)}, bf16[2,224,256]{2,1,0:T(8,128)(2,1)S(1)}, bf16[2,256,256]{2,1,0:T(8,128)(2,1)S(1)}, bf16[2,128,256]{2,1,0:T(8,128)(2,1)S(1)}) custom-call(bf16[1,512,256]{2,1,0:T(8,128)(2,1)} %k_hbm.1, bf16[1,512,256]{2,1,0:T(8,128)(2,1)} %v_hbm.1), custom_call_target="tpu_custom_call" | custom-call | tf_op jit(solution)/shard_map/pool/pallas_call | solution.py:395
  1.4 3.0 %collective-permute-start.1 = (bf16[2,224,256]{2,1,0:T(8,128)(2,1)S(1)}, bf16[2,224,256]{2,1,0:T(8,128)(2,1)S(1)}, u32[]{:S(2)}, u32[]{:S(2)}) collective-permute-start(bf16[2,224,256]{2,1,0:T(8,128)(2,1)S(1)} %get-tuple-element.33), channel_id=1, source_target_pairs={{0,4},{4,0},{8,12},{12,8},{16,20},{20,16},{24,28},{28,24},{1,5},{5... | collective-permute-start | bytes 688136 | tf_op jit(solution)/shard_map/ppermute | solution.py:369
  4.4 0.0 copy-start.1
  4.5 2.7 %collective-permute-start = (bf16[2,32,256]{2,1,0:T(8,128)(2,1)S(1)}, bf16[2,32,256]{2,1,0:T(8,128)(2,1)S(1)}, u32[]{:S(2)}, u32[]{:S(2)}) collective-permute-start(bf16[2,32,256]{2,1,0:T(8,128)(2,1)S(1)} %get-tuple-element.28.four_ref), channel_id=1, source_target_pairs={{0,16},{4,20},{8,24},{12,28},{16,0},{20,4},{24,8},{28,12},{1,17},{... | collective-permute-start | bytes 98312 | tf_op jit(solution)/shard_map/ppermute | solution.py:369
  7.1 1.3 %collective-permute-start.5 = (bf16[2,32,256]{2,1,0:T(8,128)(2,1)S(1)}, bf16[2,32,256]{2,1,0:T(8,128)(2,1)S(1)}, u32[]{:S(2)}, u32[]{:S(2)}) collective-permute-start(bf16[2,32,256]{2,1,0:T(8,128)(2,1)S(1)} %get-tuple-element.28.four_ref), channel_id=1, source_target_pairs={{0,24},{4,28},{8,16},{12,20},{16,8},{20,12},{24,0},{28,4},{1,25},{... | collective-permute-start | bytes 98312 | tf_op jit(solution)/shard_map/ppermute | solution.py:369
  8.5 0.2 collective-permute-start.2
  8.7 1.8 %collective-permute-start.3 = (bf16[2,64,256]{2,1,0:T(8,128)(2,1)S(1)}, bf16[2,64,256]{2,1,0:T(8,128)(2,1)S(1)}, u32[]{:S(2)}, u32[]{:S(2)}) collective-permute-start(bf16[2,64,256]{2,1,0:T(8,128)(2,1)S(1)} %get-tuple-element.34), channel_id=1, source_target_pairs={{0,8},{4,12},{8,0},{12,4},{16,24},{20,28},{24,16},{28,20},{1,9},{5... | collective-permute-start | bytes 196616 | tf_op jit(solution)/shard_map/ppermute | solution.py:369
  10.5 0.0 collective-permute-done.four_ref
  10.5 0.0 collective-permute-start.4
  10.5 0.0 copy-done.1
  10.5 1.5 %local.1 = (bf16[2,128,256]{2,1,0:T(8,128)(2,1)S(1)}, bf16[128,256]{1,0:T(8,128)(2,1)S(1)}, bf16[64,256]{1,0:T(8,128)(2,1)S(1)}, bf16[32,256]{1,0:T(8,128)(2,1)S(1)}, f32[3,512,256]{2,1,0:T(8,128)S(1)}) custom-call(bf16[512,256]{1,0:T(8,128)(2,1)S(1)} %bitcast.2, bf16[512,256]{1,0:T(8,128)(2,1)S(1)} %get-tuple-element.24.k_ref, ...), custom_call_target="tpu_custom_call" | custom-call | tf_op jit(solution)/shard_map/local/pallas_call | solution.py:429
  12.0 1.2 %collective-permute-done.5.six_ref = bf16[2,32,256]{2,1,0:T(8,128)(2,1)S(1)} collective-permute-done((bf16[2,32,256]{2,1,0:T(8,128)(2,1)S(1)}, bf16[2,32,256]{2,1,0:T(8,128)(2,1)S(1)}, u32[]{:S(2)}, u32[]{:S(2)}) %collective-permute-start.5) | collective-permute-done | bytes 32800 | tf_op jit(solution)/shard_map/ppermute | solution.py:369
  13.2 0.9 %collective-permute-start.6 = (bf16[2,64,256]{2,1,0:T(8,128)(2,1)S(1)}, bf16[2,64,256]{2,1,0:T(8,128)(2,1)S(1)}, u32[]{:S(2)}, u32[]{:S(2)}) collective-permute-start(bf16[2,64,256]{2,1,0:T(8,128)(2,1)S(1)} %join.1.fours_a), channel_id=1, source_target_pairs={{0,4},{4,0},{8,12},{12,8},{16,20},{20,16},{24,28},{28,24},{1,5},{5... | collective-permute-start | bytes 196616 | tf_op jit(solution)/shard_map/ppermute | solution.py:369
  14.2 0.0 collective-permute-done.2.three_a
  14.2 0.6 %collective-permute-done.3.three_b = bf16[2,64,256]{2,1,0:T(8,128)(2,1)S(1)} collective-permute-done((bf16[2,64,256]{2,1,0:T(8,128)(2,1)S(1)}, bf16[2,64,256]{2,1,0:T(8,128)(2,1)S(1)}, u32[]{:S(2)}, u32[]{:S(2)}) %collective-permute-start.3) | collective-permute-done | bytes 65568 | tf_op jit(solution)/shard_map/ppermute | solution.py:369
  14.8 0.0 collective-permute-done.1.first_ref
  14.8 0.5 %coarse.1 = (f32[3,128,256]{2,1,0:T(8,128)S(1)}, bf16[2,32,256]{2,1,0:T(8,128)(2,1)S(1)}) custom-call(bf16[128,256]{1,0:T(8,128)(2,1)S(1)} %get-tuple-element.31.two_q, bf16[64,256]{1,0:T(8,128)(2,1)S(1)} %get-tuple-element.32.three_q, bf16[2,224,256]{2,1,0:T(8,128)(2,1)S(1)} %collective-permute-done.1.first_ref, ...), custom_call_target="tpu_custom_call" | custom-call | flops 2147483648 | bytes 2097152 | tf_op jit(solution)/shard_map/coarse/pallas_call | solution.py:455
  15.3 0.0 collective-permute-done.4.second_ref
  15.3 0.0 copy-start
  15.3 0.9 %mid.1.fine = f32[2,512,256]{2,1,0:T(8,128)S(1)} custom-call(bf16[2,128,256]{2,1,0:T(8,128)(2,1)S(1)} %get-tuple-element.30.edge_q, f32[3,128,256]{2,1,0:T(8,128)S(1)} %get-tuple-element.35.coarse, f32[3,512,256]{2,1,0:T(8,128)S(1)} %get-tuple-element.36.state, bf16[2,224,256]{2,1,0:T(8,128)(2,1)S(1)} %collective-permute-done.1.first_ref, ...), custom_call_target="tpu_custom_call" | custom-call | tf_op jit(solution)/shard_map/mid/pallas_call | solution.py:471
  16.2 1.3 %collective-permute-done.6.fours_b = bf16[2,64,256]{2,1,0:T(8,128)(2,1)S(1)} collective-permute-done((bf16[2,64,256]{2,1,0:T(8,128)(2,1)S(1)}, bf16[2,64,256]{2,1,0:T(8,128)(2,1)S(1)}, u32[]{:S(2)}, u32[]{:S(2)}) %collective-permute-start.6) | collective-permute-done | bytes 65568 | tf_op jit(solution)/shard_map/ppermute | solution.py:369
  17.5 0.6 %finish.1 = (bf16[128,256]{1,0:T(8,128)(2,1)S(1)}, bf16[128,256]{1,0:T(8,128)(2,1)S(1)}, bf16[128,256]{1,0:T(8,128)(2,1)S(1)}, bf16[128,256]{1,0:T(8,128)(2,1)S(1)}) custom-call(bf16[32,256]{1,0:T(8,128)(2,1)S(1)} %get-tuple-element.29.query_ref.four_q, f32[2,512,256]{2,1,0:T(8,128)S(1)} %mid.1.fine, bf16[2,32,256]{2,1,0:T(8,128)(2,1)S(1)} %get-tuple-element.28.four_ref, ...), custom_call_target="tpu_custom_call" | custom-call | tf_op jit(solution)/shard_map/finish/pallas_call | solution.py:490
  18.1 0.1 collective-permute-start.7
  18.2 1.6 %collective-permute-start.8 = (bf16[128,256]{1,0:T(8,128)(2,1)S(1)}, bf16[128,256]{1,0:T(8,128)(2,1)S(1)}, u32[]{:S(2)}, u32[]{:S(2)}) collective-permute-start(bf16[128,256]{1,0:T(8,128)(2,1)S(1)} %get-tuple-element.41), channel_id=1, source_target_pairs={{0,2},{1,3},{2,0},{3,1},{4,6},{5,7},{6,4},{7,5},{8,10},{9,11},{10,... | collective-permute-start | bytes 196616 | tf_op jit(solution)/shard_map/ppermute | solution.py:369
  19.7 0.3 %collective-permute-start.9 = (bf16[128,256]{1,0:T(8,128)(2,1)S(1)}, bf16[128,256]{1,0:T(8,128)(2,1)S(1)}, u32[]{:S(2)}, u32[]{:S(2)}) collective-permute-start(bf16[128,256]{1,0:T(8,128)(2,1)S(1)} %get-tuple-element.42), channel_id=1, source_target_pairs={{0,1},{1,0},{2,3},{3,2},{4,5},{5,4},{6,7},{7,6},{8,9},{9,8},{10,11... | collective-permute-start | bytes 196616 | tf_op jit(solution)/shard_map/ppermute | solution.py:369
  20.0 0.0 copy-done
  20.0 0.2 partial.1.partial_ref
  20.2 2.2 %collective-permute-done.7.refs_0_ = bf16[128,256]{1,0:T(8,128)(2,1)S(1)} collective-permute-done((bf16[128,256]{1,0:T(8,128)(2,1)S(1)}, bf16[128,256]{1,0:T(8,128)(2,1)S(1)}, u32[]{:S(2)}, u32[]{:S(2)}) %collective-permute-start.7) | collective-permute-done | bytes 65568 | tf_op jit(solution)/shard_map/ppermute | solution.py:369
  22.5 1.5 %collective-permute-done.8.refs_1_ = bf16[128,256]{1,0:T(8,128)(2,1)S(1)} collective-permute-done((bf16[128,256]{1,0:T(8,128)(2,1)S(1)}, bf16[128,256]{1,0:T(8,128)(2,1)S(1)}, u32[]{:S(2)}, u32[]{:S(2)}) %collective-permute-start.8) | collective-permute-done | bytes 65568 | tf_op jit(solution)/shard_map/ppermute | solution.py:369
  23.9 0.0 collective-permute-done.9.refs_2_
  23.9 1.1 %project.1 = bf16[128,1024]{1,0:T(8,128)(2,1)} custom-call(f32[128,1024]{1,0:T(8,128)S(1)} %partial.1.partial_ref, bf16[128,256]{1,0:T(8,128)(2,1)S(1)} %collective-permute-done.7.refs_0_, bf16[128,256]{1,0:T(8,128)(2,1)S(1)} %collective-permute-done.8.refs_1_, bf16[128,256]{1,0:T(8,128)(2,1)S(1)} %collective-permute-done.9.refs_2_, ...), custom_call_target="tpu_custom_call" | custom-call | tf_op jit(solution)/shard_map/project/pallas_call | solution.py:510
  (2 shorter events, 0.0 us)
Async XLA Ops:
  1.4 13.4 %collective-permute-start.1 = (bf16[2,224,256]{2,1,0:T(8,128)(2,1)S(1)}, bf16[2,224,256]{2,1,0:T(8,128)(2,1)S(1)}, u32[]{:S(2)}, u32[]{:S(2)}) collective-permute-start(bf16[2,224,256]{2,1,0:T(8,128)(2,1)S(1)} %get-tuple-element.33), channel_id=1, source_target_pairs={{0,4},{4,0},{8,12},{12,8},{16,20},{20,16},{24,28},{28,24},{1,5},{5... | collective-permute-start | bytes 688136 | tf_op jit(solution)/shard_map/ppermute | solution.py:369
  4.4 6.0 %copy-start.1 = (bf16[1,512,256]{2,1,0:T(8,128)(2,1)S(1)}, bf16[1,512,256]{2,1,0:T(8,128)(2,1)}, u32[]{:S(2)}) copy-start(bf16[1,512,256]{2,1,0:T(8,128)(2,1)} %param.4) | copy-start | bytes 786436
  4.5 6.0 %collective-permute-start = (bf16[2,32,256]{2,1,0:T(8,128)(2,1)S(1)}, bf16[2,32,256]{2,1,0:T(8,128)(2,1)S(1)}, u32[]{:S(2)}, u32[]{:S(2)}) collective-permute-start(bf16[2,32,256]{2,1,0:T(8,128)(2,1)S(1)} %get-tuple-element.28.four_ref), channel_id=1, source_target_pairs={{0,16},{4,20},{8,24},{12,28},{16,0},{20,4},{24,8},{28,12},{1,17},{... | collective-permute-start | bytes 98312 | tf_op jit(solution)/shard_map/ppermute | solution.py:369
  7.1 6.1 %collective-permute-start.5 = (bf16[2,32,256]{2,1,0:T(8,128)(2,1)S(1)}, bf16[2,32,256]{2,1,0:T(8,128)(2,1)S(1)}, u32[]{:S(2)}, u32[]{:S(2)}) collective-permute-start(bf16[2,32,256]{2,1,0:T(8,128)(2,1)S(1)} %get-tuple-element.28.four_ref), channel_id=1, source_target_pairs={{0,24},{4,28},{8,16},{12,20},{16,8},{20,12},{24,0},{28,4},{1,25},{... | collective-permute-start | bytes 98312 | tf_op jit(solution)/shard_map/ppermute | solution.py:369
  8.5 5.7 %collective-permute-start.2 = (bf16[2,64,256]{2,1,0:T(8,128)(2,1)S(1)}, bf16[2,64,256]{2,1,0:T(8,128)(2,1)S(1)}, u32[]{:S(2)}, u32[]{:S(2)}) collective-permute-start(bf16[2,64,256]{2,1,0:T(8,128)(2,1)S(1)} %get-tuple-element.34), channel_id=1, source_target_pairs={{0,12},{4,8},{8,4},{12,0},{16,28},{20,24},{24,20},{28,16},{1,13},{... | collective-permute-start | bytes 196616 | tf_op jit(solution)/shard_map/ppermute | solution.py:369
  8.7 6.1 %collective-permute-start.3 = (bf16[2,64,256]{2,1,0:T(8,128)(2,1)S(1)}, bf16[2,64,256]{2,1,0:T(8,128)(2,1)S(1)}, u32[]{:S(2)}, u32[]{:S(2)}) collective-permute-start(bf16[2,64,256]{2,1,0:T(8,128)(2,1)S(1)} %get-tuple-element.34), channel_id=1, source_target_pairs={{0,8},{4,12},{8,0},{12,4},{16,24},{20,28},{24,16},{28,20},{1,9},{5... | collective-permute-start | bytes 196616 | tf_op jit(solution)/shard_map/ppermute | solution.py:369
  10.5 4.8 %collective-permute-start.4 = (bf16[2,128,256]{2,1,0:T(8,128)(2,1)S(1)}, bf16[2,128,256]{2,1,0:T(8,128)(2,1)S(1)}, u32[]{:S(2)}, u32[]{:S(2)}) collective-permute-start(bf16[2,128,256]{2,1,0:T(8,128)(2,1)S(1)} %get-tuple-element.37), channel_id=1, source_target_pairs={{0,1},{1,0},{2,3},{3,2},{4,8},{5,9},{6,10},{7,11},{8,4},{9,5},{10,... | collective-permute-start | bytes 393224 | tf_op jit(solution)/shard_map/ppermute | solution.py:380
  13.2 4.3 %collective-permute-start.6 = (bf16[2,64,256]{2,1,0:T(8,128)(2,1)S(1)}, bf16[2,64,256]{2,1,0:T(8,128)(2,1)S(1)}, u32[]{:S(2)}, u32[]{:S(2)}) collective-permute-start(bf16[2,64,256]{2,1,0:T(8,128)(2,1)S(1)} %join.1.fours_a), channel_id=1, source_target_pairs={{0,4},{4,0},{8,12},{12,8},{16,20},{20,16},{24,28},{28,24},{1,5},{5... | collective-permute-start | bytes 196616 | tf_op jit(solution)/shard_map/ppermute | solution.py:369
  15.3 4.7 %copy-start = (bf16[1024,1024]{1,0:T(8,128)(2,1)S(1)}, bf16[1024,1024]{1,0:T(8,128)(2,1)}, u32[]{:S(2)}) copy-start(bf16[1024,1024]{1,0:T(8,128)(2,1)} %refs_3_.1) | copy-start | bytes 6291460
  18.1 4.4 %collective-permute-start.7 = (bf16[128,256]{1,0:T(8,128)(2,1)S(1)}, bf16[128,256]{1,0:T(8,128)(2,1)S(1)}, u32[]{:S(2)}, u32[]{:S(2)}) collective-permute-start(bf16[128,256]{1,0:T(8,128)(2,1)S(1)} %get-tuple-element.40), channel_id=1, source_target_pairs={{0,3},{1,2},{2,1},{3,0},{4,7},{5,6},{6,5},{7,4},{8,11},{9,10},{10,... | collective-permute-start | bytes 196616 | tf_op jit(solution)/shard_map/ppermute | solution.py:369
  18.2 5.8 %collective-permute-start.8 = (bf16[128,256]{1,0:T(8,128)(2,1)S(1)}, bf16[128,256]{1,0:T(8,128)(2,1)S(1)}, u32[]{:S(2)}, u32[]{:S(2)}) collective-permute-start(bf16[128,256]{1,0:T(8,128)(2,1)S(1)} %get-tuple-element.41), channel_id=1, source_target_pairs={{0,2},{1,3},{2,0},{3,1},{4,6},{5,7},{6,4},{7,5},{8,10},{9,11},{10,... | collective-permute-start | bytes 196616 | tf_op jit(solution)/shard_map/ppermute | solution.py:369
  19.7 4.2 %collective-permute-start.9 = (bf16[128,256]{1,0:T(8,128)(2,1)S(1)}, bf16[128,256]{1,0:T(8,128)(2,1)S(1)}, u32[]{:S(2)}, u32[]{:S(2)}) collective-permute-start(bf16[128,256]{1,0:T(8,128)(2,1)S(1)} %get-tuple-element.42), channel_id=1, source_target_pairs={{0,1},{1,0},{2,3},{3,2},{4,5},{5,4},{6,7},{7,6},{8,9},{9,8},{10,11... | collective-permute-start | bytes 196616 | tf_op jit(solution)/shard_map/ppermute | solution.py:369

commit v3 on v2

--- a/solution.py
+++ b/solution.py
@@ -15,6 +15,8 @@
 root_half = 0.7071067811865476
 log2_e = 1.4426950408889634
 log2_scale = HD**-0.5 * log2_e
+least_share = 2.0**-100
+CORES = 2
 
 FAN = 2**LEVELS
 
@@ -231,7 +233,9 @@
             coarse[index, :, pl.ds(pair * PAIR, PAIR)] = field
 
 
-def mid_kernel(edge_q, coarse, state, first_ref, second_ref, fine, holds):
+def mid_kernel(edge_q, coarse, state, first_ref, second_ref, fine, *refs):
+    outs, (ready, holds) = refs[:-2], refs[-2:]
+    own = lax.axis_index("head")
     rows = state.shape[1]
     blocks = rows // BLOCK
     position = lax.axis_index("seq")
@@ -265,8 +269,12 @@
             for side, edge in enumerate((0, blocks - 1)):
                 if block == edge:
                     done = merged(done, weigh(holds.at[pair, side], *steps[pair, side]))
-            fine[0, here, lanes] = done[1] / done[2]
+            result = done[1] / done[2]
+            fine[0, here, lanes] = result
             fine[1, here, lanes] = done[0] + jnp.log(done[2]) * log2_e
+            ready[block, :, lanes] = result.astype(jnp.bfloat16)
+    for step, out in enumerate(outs, CORES):
+        out[...] = ready[own ^ step]
 
 
 def repeated(field):
@@ -276,10 +284,11 @@
 def finish_kernel(
     four_q, fine, four_ref, near_ref, three_a, three_b, fours_a, fours_b, *refs
 ):
-    far, refs = refs[:-6], refs[-6:]
-    outs, (attended, four_hold) = refs[:-2], refs[-2:]
-    blocks = fine.shape[1] // BLOCK
+    refs, (coarse, four_hold) = refs[:-2], refs[-2:]
+    heads = lax.axis_size("head")
+    far, outs = refs[:-heads], refs[-heads:]
     own = lax.axis_index("head")
+    features = four_q.shape[1]
     pairs = four_q.shape[1] // PAIR
     steps = {}
     for pair in range(pairs):
@@ -308,16 +317,58 @@
     for pair in range(pairs):
         lanes = pl.ds(pair * PAIR, PAIR)
         top, numer, rowsum = weigh(four_hold.at[pair], *steps[pair])
-        result, log_sum = numer / rowsum, top + jnp.log(rowsum) * log2_e
-        for block in range(blocks):
-            here = slice(block * BLOCK, (block + 1) * BLOCK)
-            few = slice(block * SLAB, (block + 1) * SLAB)
-            ours = fine[0, here, lanes]
-            keep = 1.0 / (1.0 + jnp.exp2(repeated(log_sum[few]) - fine[1, here, lanes]))
-            theirs = repeated(result[few])
-            attended[block, :, lanes] = (theirs + keep * (ours - theirs)).astype(jnp.bfloat16)
+        coarse[0, :, lanes] = numer / rowsum
+        coarse[1, :, lanes] = top + jnp.log(rowsum) * log2_e
     for step, out in enumerate(outs):
-        out[...] = attended[own ^ step]
+        block = own ^ step
+        here = pl.ds(pl.multiple_of(block * BLOCK, BLOCK), BLOCK)
+        few = pl.ds(pl.multiple_of(block * SLAB, SLAB), SLAB)
+        shares = []
+        for pair in range(pairs):
+            lanes = pl.ds(pair * PAIR, PAIR)
+            fine_sum, coarse_sum = fine[1, here, lanes], repeated(coarse[1, few, lanes])
+            if step < CORES:
+                keep = 1.0 / (1.0 + jnp.exp2(coarse_sum - fine_sum))
+                ours, theirs = fine[0, here, lanes], repeated(coarse[0, few, lanes])
+                out[:, lanes] = (theirs + keep * (ours - theirs)).astype(jnp.bfloat16)
+            else:
+                ratio = jnp.exp2(-jnp.abs(fine_sum - coarse_sum))
+                less = jnp.maximum(ratio / (1.0 + ratio), least_share)
+                shares.append(jnp.where(fine_sum <= coarse_sum, less, -less).astype(jnp.bfloat16))
+        if step >= CORES:
+            pick = lax.broadcasted_iota(jnp.int32, (2 * SLAB, features), 1) == HD * (
+                lax.broadcasted_iota(jnp.int32, (2 * SLAB, features), 0)
+            )
+            by_head = lax.dot_general(
+                pick.astype(jnp.bfloat16),
+                jnp.concatenate(shares, axis=1),
+                (((1,), (1,)), ((), ())),
+                preferred_element_type=jnp.float32,
+            )[:SLAB]
+            blank = jnp.zeros((SLAB, features - BLOCK), jnp.float32)
+            out[...] = jnp.concatenate(
+                [coarse[0, few, :], jnp.concatenate([by_head, blank], axis=1)], axis=0
+            ).astype(jnp.bfloat16)
+
+
+def rejoin_kernel(*refs):
+    outs = refs[len(refs) // 3 * 2 :]
+    for early, late_ref, out in zip(refs, refs[len(outs) :], outs):
+        features = early.shape[1]
+        late = late_ref[...].astype(jnp.float32)
+        spread = lax.broadcasted_iota(jnp.int32, (SLAB, features), 1) // HD == (
+            lax.broadcasted_iota(jnp.int32, (SLAB, features), 0)
+        )
+        signed = lax.dot_general(
+            late[SLAB:, :BLOCK].astype(jnp.bfloat16),
+            spread.astype(jnp.bfloat16),
+            (((0,), (0,)), ((), ())),
+            preferred_element_type=jnp.float32,
+        )
+        keep = jnp.where(signed >= 0, signed, 1.0 + signed)
+        join = jnp.where(signed >= 0, 1.0 - signed, -signed)
+        result = keep * early[...].astype(jnp.float32) + join * repeated(late[:SLAB])
+        out[...] = result.astype(jnp.bfloat16)
 
 
 def partial_kernel(own_ref, weight_ref, out_ref):
@@ -337,7 +388,7 @@
     for index in range(staged.shape[0]):
         columns = pl.ds(index * chunk, chunk)
         total = partial_ref[:, columns]
-        for step, part in zip(range(len(parts), 0, -1), parts):
+        for step, part in enumerate(parts, 1):
             start = pl.multiple_of((own ^ step) * features, features)
             total += jnp.dot(
                 part[...],
@@ -468,13 +519,19 @@
         cost_estimate=pl.CostEstimate(flops=2**31, bytes_accessed=2**21, transcendentals=0),
         name="coarse",
     )(two_q, three_q, first_in, *threes_in)
-    fine = pl.pallas_call(
+    away = range(CORES, head_count)
+    fine, *early = pl.pallas_call(
         mid_kernel,
-        out_shape=jax.ShapeDtypeStruct((2, rows, features), jnp.float32),
-        scratch_shapes=[pltpu.VMEM((pairs, 2, 2 * BLOCK, BLOCK), jnp.float32)],
+        out_shape=[jax.ShapeDtypeStruct((2, rows, features), jnp.float32)]
+        + [bf16(BLOCK, features) for _ in away],
+        scratch_shapes=[
+            pltpu.VMEM((rows // BLOCK, BLOCK, features), jnp.bfloat16),
+            pltpu.VMEM((pairs, 2, 2 * BLOCK, BLOCK), jnp.float32),
+        ],
         compiler_params=params,
         name="mid",
     )(edge_q, coarse, state, first_in, second_in)
+    early_in = [swapped(part, "head", step) for step, part in zip(away, early)]
 
     far = []
     known = 8
@@ -487,18 +544,19 @@
             group = jnp.concatenate([group, fresh], axis=1)
             known *= 2
 
+    near_parts = [bf16(BLOCK, features) for _ in range(CORES)]
     outs = pl.pallas_call(
         finish_kernel,
-        out_shape=[bf16(BLOCK, features) for _ in range(head_count)],
+        out_shape=near_parts + [bf16(2 * SLAB, features) for _ in away],
         scratch_shapes=[
-            pltpu.VMEM((rows // BLOCK, BLOCK, features), jnp.bfloat16),
+            pltpu.VMEM((2, rows // 16, features), jnp.float32),
             pltpu.VMEM((pairs, rows // 8, rows // 16 * seq_count), jnp.float32),
         ],
         compiler_params=params,
         name="finish",
     )(four_q, fine, four, near, *threes_in, fours, fours_in, *far)
-
-    parts = [swapped(outs[step], "head", step) for step in range(head_count - 1, 0, -1)]
+    late_in = [swapped(part, "head", step) for step, part in zip(away, outs[CORES:])]
+    near_in = swapped(outs[1], "head", 1)
     width = out_weight.shape[1]
     partial = pl.pallas_call(
         partial_kernel,
@@ -506,10 +564,17 @@
         compiler_params=params,
         name="partial",
     )(outs[0], out_weight)
+    rejoined = pl.pallas_call(
+        rejoin_kernel,
+        out_shape=[bf16(BLOCK, features) for _ in away],
+        compiler_params=params,
+        cost_estimate=pl.CostEstimate(flops=2**32, bytes_accessed=2**20, transcendentals=0),
+        name="rejoin",
+    )(*early_in, *late_in)
     chunk = 2 * PAIR
     result = pl.pallas_call(
         project_kernel,
-        in_specs=[vmem] * (len(parts) + 2),
+        in_specs=[vmem] * (3 + len(rejoined)),
         out_specs=hbm,
         out_shape=bf16(BLOCK, width),
         scratch_shapes=[
@@ -519,7 +584,7 @@
         ],
         compiler_params=params,
         name="project",
-    )(partial, *parts, out_weight)
+    )(partial, near_in, *rejoined, out_weight)
     return result[None]
 
 

time: 25.2 us -> 25.1 us (level)
  the two profiles are of different devices: /device:TPU:0 before, /device:TPU:5 now
where the time goes in v3:
time: 25.1 us; the launch traced here: 24.9 us
  starting transfers between devices  13.9 us (55%)
  Pallas kernels  6.75 us (27%)
  waiting for transfers between devices  4.15 us (17%)
    ppermute x11, starting transfers between devices, swapped(): lax.ppermute(block, axis, [(i, i ^ mask) for i in range(lax.axis_size(axi...  13.7 us
    ppermute x11, waiting for transfers between devices, swapped(): lax.ppermute(block, axis, [(i, i ^ mask) for i in range(lax.axis_size(axi...  2.21 us
    ppermute x1, waiting for transfers between devices, across(): return lax.ppermute(block, ('seq', 'head'), route)  1.94 us
    pallas_call x1, Pallas kernels, per_device(): pl.pallas_call(local_kernel, out_shape=[bf16(2, BLOCK, features), bf16(ro...  1.54 us
    pallas_call x1, Pallas kernels, per_device(): pl.pallas_call(pool_kernel, in_specs=[hbm] * 2, out_shape=[bf16(rows, fea...  1.41 us
    pallas_call x1, Pallas kernels, per_device(): pl.pallas_call(project_kernel, in_specs=[vmem] * (3 + len(rejoined)), out...  1.12 us
    pallas_call x1, Pallas kernels, per_device(): pl.pallas_call(mid_kernel, out_shape=[jax.ShapeDtypeStruct((2, rows, feat...  0.93 us
    pallas_call x1, Pallas kernels, per_device(): pl.pallas_call(finish_kernel, out_shape=near_parts + [bf16(2 * SLAB, feat...  0.7 us
  transfers between devices with their start and end apart: 12, of which 3 were waited for; matrix products, arithmetic and copies ran while one was open for 0% of the time, Pallas kernels for 17%

profile of v3, /device:TPU:5, one launch (start us, length us, event | category | flops | bytes accessed | tf_op | source)
XLA Modules:
  0.0 24.9 jit_solution(7037971183007023448)
XLA Ops:
  0.0 1.4 %pool.1 = (bf16[512,256]{1,0:T(8,128)(2,1)S(1)}, bf16[512,256]{1,0:T(8,128)(2,1)S(1)}, bf16[2,224,256]{2,1,0:T(8,128)(2,1)S(1)}, bf16[2,256,256]{2,1,0:T(8,128)(2,1)S(1)}, bf16[2,128,256]{2,1,0:T(8,128)(2,1)S(1)}) custom-call(bf16[1,512,256]{2,1,0:T(8,128)(2,1)} %k_hbm.1, bf16[1,512,256]{2,1,0:T(8,128)(2,1)} %v_hbm.1), custom_call_target="tpu_custom_call" | custom-call | tf_op jit(solution)/shard_map/pool/pallas_call | solution.py:446
  1.4 0.1 collective-permute-start.1
  1.5 0.0 copy-start.1
  1.6 2.6 %collective-permute-start = (bf16[2,32,256]{2,1,0:T(8,128)(2,1)S(1)}, bf16[2,32,256]{2,1,0:T(8,128)(2,1)S(1)}, u32[]{:S(2)}, u32[]{:S(2)}) collective-permute-start(bf16[2,32,256]{2,1,0:T(8,128)(2,1)S(1)} %get-tuple-element.33.four_ref), channel_id=1, source_target_pairs={{0,16},{4,20},{8,24},{12,28},{16,0},{20,4},{24,8},{28,12},{1,17},{... | collective-permute-start | bytes 98312 | tf_op jit(solution)/shard_map/ppermute | solution.py:420
  4.1 1.1 %collective-permute-start.5 = (bf16[2,32,256]{2,1,0:T(8,128)(2,1)S(1)}, bf16[2,32,256]{2,1,0:T(8,128)(2,1)S(1)}, u32[]{:S(2)}, u32[]{:S(2)}) collective-permute-start(bf16[2,32,256]{2,1,0:T(8,128)(2,1)S(1)} %get-tuple-element.33.four_ref), channel_id=1, source_target_pairs={{0,24},{4,28},{8,16},{12,20},{16,8},{20,12},{24,0},{28,4},{1,25},{... | collective-permute-start | bytes 98312 | tf_op jit(solution)/shard_map/ppermute | solution.py:420
  5.2 1.2 %collective-permute-start.2 = (bf16[2,64,256]{2,1,0:T(8,128)(2,1)S(1)}, bf16[2,64,256]{2,1,0:T(8,128)(2,1)S(1)}, u32[]{:S(2)}, u32[]{:S(2)}) collective-permute-start(bf16[2,64,256]{2,1,0:T(8,128)(2,1)S(1)} %get-tuple-element.39), channel_id=1, source_target_pairs={{0,12},{4,8},{8,4},{12,0},{16,28},{20,24},{24,20},{28,16},{1,13},{... | collective-permute-start | bytes 196616 | tf_op jit(solution)/shard_map/ppermute | solution.py:420
  6.4 1.3 %collective-permute-start.3 = (bf16[2,64,256]{2,1,0:T(8,128)(2,1)S(1)}, bf16[2,64,256]{2,1,0:T(8,128)(2,1)S(1)}, u32[]{:S(2)}, u32[]{:S(2)}) collective-permute-start(bf16[2,64,256]{2,1,0:T(8,128)(2,1)S(1)} %get-tuple-element.39), channel_id=1, source_target_pairs={{0,8},{4,12},{8,0},{12,4},{16,24},{20,28},{24,16},{28,20},{1,9},{5... | collective-permute-start | bytes 196616 | tf_op jit(solution)/shard_map/ppermute | solution.py:420
  7.6 0.0 collective-permute-done.four_ref
  7.6 0.2 collective-permute-start.4
  7.8 0.0 copy-done.1
  7.8 1.5 %local.1 = (bf16[2,128,256]{2,1,0:T(8,128)(2,1)S(1)}, bf16[128,256]{1,0:T(8,128)(2,1)S(1)}, bf16[64,256]{1,0:T(8,128)(2,1)S(1)}, bf16[32,256]{1,0:T(8,128)(2,1)S(1)}, f32[3,512,256]{2,1,0:T(8,128)S(1)}) custom-call(bf16[512,256]{1,0:T(8,128)(2,1)S(1)} %bitcast.2, bf16[512,256]{1,0:T(8,128)(2,1)S(1)} %get-tuple-element.29.k_ref, ...), custom_call_target="tpu_custom_call" | custom-call | tf_op jit(solution)/shard_map/local/pallas_call | solution.py:480
  9.3 0.0 collective-permute-done.5.six_ref
  9.4 2.2 %collective-permute-start.6 = (bf16[2,64,256]{2,1,0:T(8,128)(2,1)S(1)}, bf16[2,64,256]{2,1,0:T(8,128)(2,1)S(1)}, u32[]{:S(2)}, u32[]{:S(2)}) collective-permute-start(bf16[2,64,256]{2,1,0:T(8,128)(2,1)S(1)} %join.1.fours_a), channel_id=1, source_target_pairs={{0,4},{4,0},{8,12},{12,8},{16,20},{20,16},{24,28},{28,24},{1,5},{5... | collective-permute-start | bytes 196616 | tf_op jit(solution)/shard_map/ppermute | solution.py:420
  11.6 0.0 collective-permute-done.2.three_a
  11.6 0.0 collective-permute-done.3.three_b
  11.6 0.0 collective-permute-done.1.first_ref
  11.6 0.5 %coarse.1 = (f32[3,128,256]{2,1,0:T(8,128)S(1)}, bf16[2,32,256]{2,1,0:T(8,128)(2,1)S(1)}) custom-call(bf16[128,256]{1,0:T(8,128)(2,1)S(1)} %get-tuple-element.36.two_q, bf16[64,256]{1,0:T(8,128)(2,1)S(1)} %get-tuple-element.37.three_q, bf16[2,224,256]{2,1,0:T(8,128)(2,1)S(1)} %collective-permute-done.1.first_ref, ...), custom_call_target="tpu_custom_call" | custom-call | flops 2147483648 | bytes 2097152 | tf_op jit(solution)/shard_map/coarse/pallas_call | solution.py:506
  12.1 0.0 copy-start
  12.1 1.9 %collective-permute-done.4.second_ref = bf16[2,128,256]{2,1,0:T(8,128)(2,1)S(1)} collective-permute-done((bf16[2,128,256]{2,1,0:T(8,128)(2,1)S(1)}, bf16[2,128,256]{2,1,0:T(8,128)(2,1)S(1)}, u32[]{:S(2)}, u32[]{:S(2)}) %collective-permute-start.4) | collective-permute-done | bytes 131104 | tf_op jit(solution)/shard_map/ppermute | solution.py:431
  14.0 0.9 %mid.1 = (f32[2,512,256]{2,1,0:T(8,128)S(1)}, bf16[128,256]{1,0:T(8,128)(2,1)S(1)}, bf16[128,256]{1,0:T(8,128)(2,1)S(1)}) custom-call(bf16[2,128,256]{2,1,0:T(8,128)(2,1)S(1)} %get-tuple-element.35.edge_q, f32[3,128,256]{2,1,0:T(8,128)S(1)} %get-tuple-element.40.coarse, f32[3,512,256]{2,1,0:T(8,128)S(1)} %get-tuple-element.41.state, ...), custom_call_target="tpu_custom_call" | custom-call | tf_op jit(solution)/shard_map/mid/pallas_call | solution.py:523
  15.0 1.3 %collective-permute-start.8 = (bf16[128,256]{1,0:T(8,128)(2,1)S(1)}, bf16[128,256]{1,0:T(8,128)(2,1)S(1)}, u32[]{:S(2)}, u32[]{:S(2)}) collective-permute-start(bf16[128,256]{1,0:T(8,128)(2,1)S(1)} %get-tuple-element.47), channel_id=1, source_target_pairs={{0,2},{1,3},{2,0},{3,1},{4,6},{5,7},{6,4},{7,5},{8,10},{9,11},{10,... | collective-permute-start | bytes 196616 | tf_op jit(solution)/shard_map/ppermute | solution.py:420
  16.3 2.2 %collective-permute-start.9 = (bf16[128,256]{1,0:T(8,128)(2,1)S(1)}, bf16[128,256]{1,0:T(8,128)(2,1)S(1)}, u32[]{:S(2)}, u32[]{:S(2)}) collective-permute-start(bf16[128,256]{1,0:T(8,128)(2,1)S(1)} %get-tuple-element.48), channel_id=1, source_target_pairs={{0,3},{1,2},{2,1},{3,0},{4,7},{5,6},{6,5},{7,4},{8,11},{9,10},{10,... | collective-permute-start | bytes 196616 | tf_op jit(solution)/shard_map/ppermute | solution.py:420
  18.5 0.0 collective-permute-done.6.fours_b
  18.5 0.7 %finish.1 = (bf16[128,256]{1,0:T(8,128)(2,1)S(1)}, bf16[128,256]{1,0:T(8,128)(2,1)S(1)}, bf16[16,256]{1,0:T(8,128)(2,1)S(1)}, bf16[16,256]{1,0:T(8,128)(2,1)S(1)}) custom-call(bf16[32,256]{1,0:T(8,128)(2,1)S(1)} %get-tuple-element.34.query_ref.four_q, f32[2,512,256]{2,1,0:T(8,128)S(1)} %get-tuple-element.43.fine, ...), custom_call_target="tpu_custom_call" | custom-call | tf_op jit(solution)/shard_map/finish/pallas_call | solution.py:548
  19.2 1.2 %collective-permute-start.10 = (bf16[16,256]{1,0:T(8,128)(2,1)S(1)}, bf16[16,256]{1,0:T(8,128)(2,1)S(1)}, u32[]{:S(2)}, u32[]{:S(2)}) collective-permute-start(bf16[16,256]{1,0:T(8,128)(2,1)S(1)} %get-tuple-element.49), channel_id=1, source_target_pairs={{0,2},{1,3},{2,0},{3,1},{4,6},{5,7},{6,4},{7,5},{8,10},{9,11},{10,... | collective-permute-start | bytes 24584 | tf_op jit(solution)/shard_map/ppermute | solution.py:420
  20.4 0.3 %collective-permute-start.11 = (bf16[16,256]{1,0:T(8,128)(2,1)S(1)}, bf16[16,256]{1,0:T(8,128)(2,1)S(1)}, u32[]{:S(2)}, u32[]{:S(2)}) collective-permute-start(bf16[16,256]{1,0:T(8,128)(2,1)S(1)} %get-tuple-element.50), channel_id=1, source_target_pairs={{0,3},{1,2},{2,1},{3,0},{4,7},{5,6},{6,5},{7,4},{8,11},{9,10},{10,... | collective-permute-start | bytes 24584 | tf_op jit(solution)/shard_map/ppermute | solution.py:420
  20.7 0.4 %collective-permute-start.7 = (bf16[128,256]{1,0:T(8,128)(2,1)S(1)}, bf16[128,256]{1,0:T(8,128)(2,1)S(1)}, u32[]{:S(2)}, u32[]{:S(2)}) collective-permute-start(bf16[128,256]{1,0:T(8,128)(2,1)S(1)} %get-tuple-element.46), channel_id=1, source_target_pairs={{0,1},{1,0},{2,3},{3,2},{4,5},{5,4},{6,7},{7,6},{8,9},{9,8},{10,11... | collective-permute-start | bytes 196616 | tf_op jit(solution)/shard_map/ppermute | solution.py:420
  21.1 0.0 copy-done
  21.1 0.2 partial.1.partial_ref
  21.3 0.8 %collective-permute-done.10.refs_2_ = bf16[16,256]{1,0:T(8,128)(2,1)S(1)} collective-permute-done((bf16[16,256]{1,0:T(8,128)(2,1)S(1)}, bf16[16,256]{1,0:T(8,128)(2,1)S(1)}, u32[]{:S(2)}, u32[]{:S(2)}) %collective-permute-start.10) | collective-permute-done | bytes 8224 | tf_op jit(solution)/shard_map/ppermute | solution.py:420
  22.1 1.4 %collective-permute-done.11.refs_3_ = bf16[16,256]{1,0:T(8,128)(2,1)S(1)} collective-permute-done((bf16[16,256]{1,0:T(8,128)(2,1)S(1)}, bf16[16,256]{1,0:T(8,128)(2,1)S(1)}, u32[]{:S(2)}, u32[]{:S(2)}) %collective-permute-start.11) | collective-permute-done | bytes 8224 | tf_op jit(solution)/shard_map/ppermute | solution.py:420
  23.5 0.0 collective-permute-done.8.refs_0_
  23.5 0.0 collective-permute-done.9.refs_1_
  23.5 0.3 %rejoin.1 = (bf16[128,256]{1,0:T(8,128)(2,1)S(1)}, bf16[128,256]{1,0:T(8,128)(2,1)S(1)}) custom-call(bf16[128,256]{1,0:T(8,128)(2,1)S(1)} %collective-permute-done.8.refs_0_, bf16[128,256]{1,0:T(8,128)(2,1)S(1)} %collective-permute-done.9.refs_1_, bf16[16,256]{1,0:T(8,128)(2,1)S(1)} %collective-permute-done.10.refs_2_, ...), custom_call_target="tpu_custom_call" | custom-call | flops 4294967296 | bytes 1048576 | tf_op jit(solution)/shard_map/rejoin/pallas_call | solution.py:567
  23.8 0.0 collective-permute-done.7.refs_0_
  23.8 1.1 %project.1 = bf16[128,1024]{1,0:T(8,128)(2,1)} custom-call(f32[128,1024]{1,0:T(8,128)S(1)} %partial.1.partial_ref, bf16[128,256]{1,0:T(8,128)(2,1)S(1)} %collective-permute-done.7.refs_0_, bf16[128,256]{1,0:T(8,128)(2,1)S(1)} %get-tuple-element.51.refs_1_, bf16[128,256]{1,0:T(8,128)(2,1)S(1)} %get-tuple-element.52.refs_2_, bf16[1024,1024]{1,0:T(8,128)(2,1)S(1)} %copy-done), custom_call_target="tpu_custom_call" | custom-call | tf_op jit(solution)/shard_map/project/pallas_call | solution.py:575
  (2 shorter events, 0.1 us)
Async XLA Ops:
  1.4 10.2 %collective-permute-start.1 = (bf16[2,224,256]{2,1,0:T(8,128)(2,1)S(1)}, bf16[2,224,256]{2,1,0:T(8,128)(2,1)S(1)}, u32[]{:S(2)}, u32[]{:S(2)}) collective-permute-start(bf16[2,224,256]{2,1,0:T(8,128)(2,1)S(1)} %get-tuple-element.38), channel_id=1, source_target_pairs={{0,4},{4,0},{8,12},{12,8},{16,20},{20,16},{24,28},{28,24},{1,5},{5... | collective-permute-start | bytes 688136 | tf_op jit(solution)/shard_map/ppermute | solution.py:420
  1.5 6.3 %copy-start.1 = (bf16[1,512,256]{2,1,0:T(8,128)(2,1)S(1)}, bf16[1,512,256]{2,1,0:T(8,128)(2,1)}, u32[]{:S(2)}) copy-start(bf16[1,512,256]{2,1,0:T(8,128)(2,1)} %param.4) | copy-start | bytes 786436
  1.6 6.1 %collective-permute-start = (bf16[2,32,256]{2,1,0:T(8,128)(2,1)S(1)}, bf16[2,32,256]{2,1,0:T(8,128)(2,1)S(1)}, u32[]{:S(2)}, u32[]{:S(2)}) collective-permute-start(bf16[2,32,256]{2,1,0:T(8,128)(2,1)S(1)} %get-tuple-element.33.four_ref), channel_id=1, source_target_pairs={{0,16},{4,20},{8,24},{12,28},{16,0},{20,4},{24,8},{28,12},{1,17},{... | collective-permute-start | bytes 98312 | tf_op jit(solution)/shard_map/ppermute | solution.py:420
  4.1 5.2 %collective-permute-start.5 = (bf16[2,32,256]{2,1,0:T(8,128)(2,1)S(1)}, bf16[2,32,256]{2,1,0:T(8,128)(2,1)S(1)}, u32[]{:S(2)}, u32[]{:S(2)}) collective-permute-start(bf16[2,32,256]{2,1,0:T(8,128)(2,1)S(1)} %get-tuple-element.33.four_ref), channel_id=1, source_target_pairs={{0,24},{4,28},{8,16},{12,20},{16,8},{20,12},{24,0},{28,4},{1,25},{... | collective-permute-start | bytes 98312 | tf_op jit(solution)/shard_map/ppermute | solution.py:420
  5.2 6.4 %collective-permute-start.2 = (bf16[2,64,256]{2,1,0:T(8,128)(2,1)S(1)}, bf16[2,64,256]{2,1,0:T(8,128)(2,1)S(1)}, u32[]{:S(2)}, u32[]{:S(2)}) collective-permute-start(bf16[2,64,256]{2,1,0:T(8,128)(2,1)S(1)} %get-tuple-element.39), channel_id=1, source_target_pairs={{0,12},{4,8},{8,4},{12,0},{16,28},{20,24},{24,20},{28,16},{1,13},{... | collective-permute-start | bytes 196616 | tf_op jit(solution)/shard_map/ppermute | solution.py:420
  6.4 5.2 %collective-permute-start.3 = (bf16[2,64,256]{2,1,0:T(8,128)(2,1)S(1)}, bf16[2,64,256]{2,1,0:T(8,128)(2,1)S(1)}, u32[]{:S(2)}, u32[]{:S(2)}) collective-permute-start(bf16[2,64,256]{2,1,0:T(8,128)(2,1)S(1)} %get-tuple-element.39), channel_id=1, source_target_pairs={{0,8},{4,12},{8,0},{12,4},{16,24},{20,28},{24,16},{28,20},{1,9},{5... | collective-permute-start | bytes 196616 | tf_op jit(solution)/shard_map/ppermute | solution.py:420
  7.6 6.4 %collective-permute-start.4 = (bf16[2,128,256]{2,1,0:T(8,128)(2,1)S(1)}, bf16[2,128,256]{2,1,0:T(8,128)(2,1)S(1)}, u32[]{:S(2)}, u32[]{:S(2)}) collective-permute-start(bf16[2,128,256]{2,1,0:T(8,128)(2,1)S(1)} %get-tuple-element.42), channel_id=1, source_target_pairs={{0,1},{1,0},{2,3},{3,2},{4,8},{5,9},{6,10},{7,11},{8,4},{9,5},{10,... | collective-permute-start | bytes 393224 | tf_op jit(solution)/shard_map/ppermute | solution.py:431
  9.4 9.1 %collective-permute-start.6 = (bf16[2,64,256]{2,1,0:T(8,128)(2,1)S(1)}, bf16[2,64,256]{2,1,0:T(8,128)(2,1)S(1)}, u32[]{:S(2)}, u32[]{:S(2)}) collective-permute-start(bf16[2,64,256]{2,1,0:T(8,128)(2,1)S(1)} %join.1.fours_a), channel_id=1, source_target_pairs={{0,4},{4,0},{8,12},{12,8},{16,20},{20,16},{24,28},{28,24},{1,5},{5... | collective-permute-start | bytes 196616 | tf_op jit(solution)/shard_map/ppermute | solution.py:420
  12.1 9.0 %copy-start = (bf16[1024,1024]{1,0:T(8,128)(2,1)S(1)}, bf16[1024,1024]{1,0:T(8,128)(2,1)}, u32[]{:S(2)}) copy-start(bf16[1024,1024]{1,0:T(8,128)(2,1)} %refs_3_.1) | copy-start | bytes 6291460
  15.0 8.5 %collective-permute-start.8 = (bf16[128,256]{1,0:T(8,128)(2,1)S(1)}, bf16[128,256]{1,0:T(8,128)(2,1)S(1)}, u32[]{:S(2)}, u32[]{:S(2)}) collective-permute-start(bf16[128,256]{1,0:T(8,128)(2,1)S(1)} %get-tuple-element.47), channel_id=1, source_target_pairs={{0,2},{1,3},{2,0},{3,1},{4,6},{5,7},{6,4},{7,5},{8,10},{9,11},{10,... | collective-permute-start | bytes 196616 | tf_op jit(solution)/shard_map/ppermute | solution.py:420
  16.3 7.2 %collective-permute-start.9 = (bf16[128,256]{1,0:T(8,128)(2,1)S(1)}, bf16[128,256]{1,0:T(8,128)(2,1)S(1)}, u32[]{:S(2)}, u32[]{:S(2)}) collective-permute-start(bf16[128,256]{1,0:T(8,128)(2,1)S(1)} %get-tuple-element.48), channel_id=1, source_target_pairs={{0,3},{1,2},{2,1},{3,0},{4,7},{5,6},{6,5},{7,4},{8,11},{9,10},{10,... | collective-permute-start | bytes 196616 | tf_op jit(solution)/shard_map/ppermute | solution.py:420
  19.2 2.9 %collective-permute-start.10 = (bf16[16,256]{1,0:T(8,128)(2,1)S(1)}, bf16[16,256]{1,0:T(8,128)(2,1)S(1)}, u32[]{:S(2)}, u32[]{:S(2)}) collective-permute-start(bf16[16,256]{1,0:T(8,128)(2,1)S(1)} %get-tuple-element.49), channel_id=1, source_target_pairs={{0,2},{1,3},{2,0},{3,1},{4,6},{5,7},{6,4},{7,5},{8,10},{9,11},{10,... | collective-permute-start | bytes 24584 | tf_op jit(solution)/shard_map/ppermute | solution.py:420
  20.4 3.1 %collective-permute-start.11 = (bf16[16,256]{1,0:T(8,128)(2,1)S(1)}, bf16[16,256]{1,0:T(8,128)(2,1)S(1)}, u32[]{:S(2)}, u32[]{:S(2)}) collective-permute-start(bf16[16,256]{1,0:T(8,128)(2,1)S(1)} %get-tuple-element.50), channel_id=1, source_target_pairs={{0,3},{1,2},{2,1},{3,0},{4,7},{5,6},{6,5},{7,4},{8,11},{9,10},{10,... | collective-permute-start | bytes 24584 | tf_op jit(solution)/shard_map/ppermute | solution.py:420
  20.7 3.1 %collective-permute-start.7 = (bf16[128,256]{1,0:T(8,128)(2,1)S(1)}, bf16[128,256]{1,0:T(8,128)(2,1)S(1)}, u32[]{:S(2)}, u32[]{:S(2)}) collective-permute-start(bf16[128,256]{1,0:T(8,128)(2,1)S(1)} %get-tuple-element.46), channel_id=1, source_target_pairs={{0,1},{1,0},{2,3},{3,2},{4,5},{5,4},{6,7},{7,6},{8,9},{9,8},{10,11... | collective-permute-start | bytes 196616 | tf_op jit(solution)/shard_map/ppermute | solution.py:420
